TPU v7x, 32 devices: a whole 2x2x4 slice. The times are simulated.
32 devices in a mesh: gx: 4 (over z), gy: 8 (over y, x, core).
Axes of the slice: x: 2, y: 2, z: 4, core: 2. Of those that a mesh axis runs over, the one named last changes fastest.
Arguments:
- cube_tokens: bfloat16 [64, 1536, 768], P(('gx', 'gy')), may hold values from -6 to 6
- visible: int32 [64, 384], P(('gx', 'gy')), may hold values from 0 to 1535, as said below
- padding: int32 [64, 384], P(('gx', 'gy')), may hold values from 0 to 1, as said below
- attend_gain: bfloat16 [768], P(('gx', 'gy')), may hold values from 0.5 to 1.5
- attend_shift: bfloat16 [768], P(('gx', 'gy')), may hold values from -3 to 3
- triple_weight: bfloat16 [768, 2304], P(('gx', 'gy')), may hold values from -0.21875 to 0.21875
- query_bias: bfloat16 [768], P(('gx', 'gy')), may hold values from -3 to 3
- value_bias: bfloat16 [768], P(('gx', 'gy')), may hold values from -3 to 3
- merge_weight: bfloat16 [768, 768], P(('gx', 'gy')), may hold values from -1.25 to 1.25
- merge_bias: bfloat16 [768], P(('gx', 'gy')), may hold values from -3 to 3
- feed_gain: bfloat16 [768], P(('gx', 'gy')), may hold values from 0.5 to 1.5
- feed_shift: bfloat16 [768], P(('gx', 'gy')), may hold values from -3 to 3
- up_weight: bfloat16 [768, 3072], P(('gx', 'gy')), may hold values from -0.21875 to 0.21875
- up_bias: bfloat16 [3072], P(('gx', 'gy')), may hold values from -3 to 3
- down_weight: bfloat16 [3072, 768], P(('gx', 'gy')), may hold values from -0.109375 to 0.109375
- down_bias: bfloat16 [768], P(('gx', 'gy')), may hold values from -3 to 3
- cotangent: bfloat16 [64, 384, 768], P(('gx', 'gy')), may hold values from -6 to 6
Outputs:
- block_output: float32 [64, 384, 768], P(('gx', 'gy'))
- cube_gradient: float32 [64, 1536, 768], P(('gx', 'gy'))
- attend_gain_gradient: float32 [768], P(('gx', 'gy'))
- attend_shift_gradient: float32 [768], P(('gx', 'gy'))
- triple_weight_gradient: float32 [768, 2304], P(('gx', 'gy'))
- query_bias_gradient: float32 [768], P(('gx', 'gy'))
- value_bias_gradient: float32 [768], P(('gx', 'gy'))
- merge_weight_gradient: float32 [768, 768], P(('gx', 'gy'))
- merge_bias_gradient: float32 [768], P(('gx', 'gy'))
- feed_gain_gradient: float32 [768], P(('gx', 'gy'))
- feed_shift_gradient: float32 [768], P(('gx', 'gy'))
- up_weight_gradient: float32 [768, 3072], P(('gx', 'gy'))
- up_bias_gradient: float32 [3072], P(('gx', 'gy'))
- down_weight_gradient: float32 [3072, 768], P(('gx', 'gy'))
- down_bias_gradient: float32 [768], P(('gx', 'gy'))
Inputs may be any that keep to these rules, and one draw needn't show every extreme that they name: `visible`: the 384 positions of a sample are distinct. `padding`: each sample's row is 1 on a leading run of slots and 0 after it; the run holds 154 to 384 slots, except that the last slot of a device may hold no sample (all 0), so a device holds 1 or 2 samples; some sample fills all 384 slots.
All inputs are finite; a program needn't handle non-finite values.
Results may differ from a plain program's by a relative error of at most 0.013.
Values may be sent and summed in bfloat16 or wider, within the bound.
No kernel may reach another device: no remote copies, remote signals or barrier semaphores. Data moves between devices by JAX's collectives and lax.ppermute only.
A program may use at most 192 MiB of HBM per device.

v0:
```python
import jax
import jax.numpy as jnp
from jax import lax
from jax.sharding import PartitionSpec as P

HEADS = 12
HEAD = 64


epsilon = 1e-06


def normalize(values, gain, shift):
    center = values - jnp.mean(values, axis=-1, keepdims=True)
    scale = lax.rsqrt(jnp.mean(center * center, axis=-1, keepdims=True) + epsilon)
    normed = center * scale
    return (normed * gain + shift, normed, scale)


def normalize_back(grad_out, normed, scale, gain):
    gain_term = jnp.sum(grad_out * normed, axis=(0, 1))
    shift_term = jnp.sum(grad_out, axis=(0, 1))
    inner = grad_out * gain
    grad_in = scale * (
        inner
        - jnp.mean(inner, axis=-1, keepdims=True)
        - normed * jnp.mean(inner * normed, axis=-1, keepdims=True)
    )
    return (grad_in, gain_term, shift_term)


def fetch_weights(
    attend_gain,
    attend_shift,
    triple_weight,
    query_bias,
    value_bias,
    merge_weight,
    merge_bias,
    feed_gain,
    feed_shift,
    up_weight,
    up_bias,
    down_weight,
    down_bias,
):
    whole = (
        lax.all_gather(attend_gain, ("gx", "gy"), axis=0, tiled=True),
        lax.all_gather(attend_shift, ("gx", "gy"), axis=0, tiled=True),
        lax.all_gather(triple_weight, ("gx", "gy"), axis=0, tiled=True),
        lax.all_gather(query_bias, ("gx", "gy"), axis=0, tiled=True),
        lax.all_gather(value_bias, ("gx", "gy"), axis=0, tiled=True),
        lax.all_gather(merge_weight, ("gx", "gy"), axis=0, tiled=True),
        lax.all_gather(merge_bias, ("gx", "gy"), axis=0, tiled=True),
        lax.all_gather(feed_gain, ("gx", "gy"), axis=0, tiled=True),
        lax.all_gather(feed_shift, ("gx", "gy"), axis=0, tiled=True),
        lax.all_gather(up_weight, ("gx", "gy"), axis=0, tiled=True),
        lax.all_gather(up_bias, ("gx", "gy"), axis=0, tiled=True),
        lax.all_gather(down_weight, ("gx", "gy"), axis=0, tiled=True),
        lax.all_gather(down_bias, ("gx", "gy"), axis=0, tiled=True),
    )
    return whole


def reduce_gradients(grads):
    summed = (
        lax.psum_scatter(grads[0], ("gx", "gy"), scatter_dimension=0, tiled=True),
        lax.psum_scatter(grads[1], ("gx", "gy"), scatter_dimension=0, tiled=True),
        lax.psum_scatter(grads[2], ("gx", "gy"), scatter_dimension=0, tiled=True),
        lax.psum_scatter(grads[3], ("gx", "gy"), scatter_dimension=0, tiled=True),
        lax.psum_scatter(grads[4], ("gx", "gy"), scatter_dimension=0, tiled=True),
        lax.psum_scatter(grads[5], ("gx", "gy"), scatter_dimension=0, tiled=True),
        lax.psum_scatter(grads[6], ("gx", "gy"), scatter_dimension=0, tiled=True),
        lax.psum_scatter(grads[7], ("gx", "gy"), scatter_dimension=0, tiled=True),
        lax.psum_scatter(grads[8], ("gx", "gy"), scatter_dimension=0, tiled=True),
        lax.psum_scatter(grads[9], ("gx", "gy"), scatter_dimension=0, tiled=True),
        lax.psum_scatter(grads[10], ("gx", "gy"), scatter_dimension=0, tiled=True),
        lax.psum_scatter(grads[11], ("gx", "gy"), scatter_dimension=0, tiled=True),
        lax.psum_scatter(grads[12], ("gx", "gy"), scatter_dimension=0, tiled=True),
    )
    return summed


def attention_scores(queries, keys_all, keep):
    scores = (
        jnp.einsum("slhe,smhe->shlm", queries, keys_all, preferred_element_type=jnp.float32) * 0.125
    )
    return jnp.where(keep[:, None, None, :] > 0, scores, -1000000000.0)


def forward_pass(rows, keep, weights):
    (
        attend_gain,
        attend_shift,
        triple_weight,
        query_bias,
        value_bias,
        merge_weight,
        merge_bias,
        feed_gain,
        feed_shift,
        up_weight,
        up_bias,
        down_weight,
        down_bias,
    ) = weights
    slots, length, width = rows.shape
    first_out, first_normed, first_scale = normalize(
        rows, attend_gain.astype(jnp.float32), attend_shift.astype(jnp.float32)
    )
    first_low = first_out.astype(jnp.bfloat16).reshape(slots * length, width)
    joint_bias = jnp.concatenate(
        [
            query_bias.astype(jnp.float32),
            jnp.zeros((width,), jnp.float32),
            value_bias.astype(jnp.float32),
        ]
    )
    triple = jnp.dot(first_low, triple_weight, preferred_element_type=jnp.float32) + joint_bias
    triple = triple.astype(jnp.bfloat16).reshape(slots, length, 3, HEADS, HEAD)
    scores = attention_scores(triple[:, :, 0], triple[:, :, 1], keep)
    peak = jnp.max(scores, axis=-1, keepdims=True)
    expo = jnp.exp(scores - peak)
    total = jnp.sum(expo, axis=-1, keepdims=True)
    probs_low = (expo / total).astype(jnp.bfloat16)
    logsum = peak + jnp.log(total)
    mixed = jnp.einsum(
        "shlm,smhe->slhe", probs_low, triple[:, :, 2], preferred_element_type=jnp.float32
    )
    mixed = mixed.reshape(slots * length, width).astype(jnp.bfloat16)
    attended = jnp.dot(mixed, merge_weight, preferred_element_type=jnp.float32) + merge_bias.astype(
        jnp.float32
    )
    middle = rows + attended.reshape(slots, length, width)
    second_out, second_normed, second_scale = normalize(
        middle, feed_gain.astype(jnp.float32), feed_shift.astype(jnp.float32)
    )
    second_low = second_out.astype(jnp.bfloat16).reshape(slots * length, width)
    hidden = jnp.dot(second_low, up_weight, preferred_element_type=jnp.float32) + up_bias.astype(
        jnp.float32
    )
    active = jax.nn.gelu(hidden, approximate=False).astype(jnp.bfloat16)
    branch = jnp.dot(active, down_weight, preferred_element_type=jnp.float32) + down_bias.astype(
        jnp.float32
    )
    result = (middle + branch.reshape(slots, length, width)) * keep[:, :, None]
    saved = (
        first_normed,
        first_scale,
        first_low,
        triple,
        logsum,
        mixed,
        second_normed,
        second_scale,
        second_low,
        hidden,
        active,
    )
    return (result, saved)


def backward_pass(keep, weights, saved, cotangent):
    (
        attend_gain,
        attend_shift,
        triple_weight,
        query_bias,
        value_bias,
        merge_weight,
        merge_bias,
        feed_gain,
        feed_shift,
        up_weight,
        up_bias,
        down_weight,
        down_bias,
    ) = weights
    (
        first_normed,
        first_scale,
        first_low,
        triple,
        logsum,
        mixed,
        second_normed,
        second_scale,
        second_low,
        hidden,
        active,
    ) = saved
    slots, length = keep.shape
    width = first_normed.shape[2]
    flat_rows = slots * length
    grad_out = cotangent.astype(jnp.float32) * keep[:, :, None]
    grad_low = grad_out.astype(jnp.bfloat16).reshape(flat_rows, width)
    down_weight_grad = jnp.einsum("rf,rd->fd", active, grad_low, preferred_element_type=jnp.float32)
    down_bias_grad = jnp.sum(grad_out, axis=(0, 1))
    grad_active = jnp.einsum("rd,fd->rf", grad_low, down_weight, preferred_element_type=jnp.float32)
    normal_cdf = 0.5 * (1.0 + jax.scipy.special.erf(hidden * 0.7071067811865476))
    normal_density = jnp.exp(-0.5 * hidden * hidden) * 0.3989422804014327
    grad_hidden = (grad_active * (normal_cdf + hidden * normal_density)).astype(jnp.bfloat16)
    up_weight_grad = jnp.einsum(
        "rd,rf->df", second_low, grad_hidden, preferred_element_type=jnp.float32
    )
    up_bias_grad = jnp.sum(grad_hidden.astype(jnp.float32), axis=0)
    grad_second = jnp.einsum(
        "rf,df->rd", grad_hidden, up_weight, preferred_element_type=jnp.float32
    )
    grad_norm_two, feed_gain_grad, feed_shift_grad = normalize_back(
        grad_second.reshape(slots, length, width),
        second_normed,
        second_scale,
        feed_gain.astype(jnp.float32),
    )
    grad_middle = grad_out + grad_norm_two
    grad_branch = grad_middle.astype(jnp.bfloat16).reshape(flat_rows, width)
    merge_weight_grad = jnp.einsum(
        "rd,re->de", mixed, grad_branch, preferred_element_type=jnp.float32
    )
    merge_bias_grad = jnp.sum(grad_branch.astype(jnp.float32), axis=0)
    grad_mixed = jnp.einsum(
        "re,de->rd", grad_branch, merge_weight, preferred_element_type=jnp.float32
    )
    grad_mixed = grad_mixed.astype(jnp.bfloat16).reshape(slots, length, HEADS, HEAD)
    queries = triple[:, :, 0]
    keys_all = triple[:, :, 1]
    values_all = triple[:, :, 2]
    probs = jnp.exp(attention_scores(queries, keys_all, keep) - logsum)
    probs_low = probs.astype(jnp.bfloat16)
    grad_values = jnp.einsum(
        "shlm,slhe->smhe", probs_low, grad_mixed, preferred_element_type=jnp.float32
    )
    grad_probs = jnp.einsum(
        "slhe,smhe->shlm", grad_mixed, values_all, preferred_element_type=jnp.float32
    )
    grad_scores = probs * (grad_probs - jnp.sum(grad_probs * probs, axis=-1, keepdims=True))
    grad_scores = grad_scores.astype(jnp.bfloat16)
    grad_queries = (
        jnp.einsum("shlm,smhe->slhe", grad_scores, keys_all, preferred_element_type=jnp.float32)
        * 0.125
    )
    grad_keys = (
        jnp.einsum("shlm,slhe->smhe", grad_scores, queries, preferred_element_type=jnp.float32)
        * 0.125
    )
    grad_triple = jnp.stack([grad_queries, grad_keys, grad_values], axis=2)
    grad_triple = grad_triple.reshape(flat_rows, 3 * width).astype(jnp.bfloat16)
    triple_weight_grad = jnp.einsum(
        "rd,re->de", first_low, grad_triple, preferred_element_type=jnp.float32
    )
    triple_sums = jnp.sum(grad_triple.astype(jnp.float32), axis=0)
    query_bias_grad = triple_sums[:width]
    value_bias_grad = triple_sums[2 * width :]
    grad_first = jnp.einsum(
        "re,de->rd", grad_triple, triple_weight, preferred_element_type=jnp.float32
    )
    grad_norm_one, attend_gain_grad, attend_shift_grad = normalize_back(
        grad_first.reshape(slots, length, width),
        first_normed,
        first_scale,
        attend_gain.astype(jnp.float32),
    )
    grad_rows = grad_middle + grad_norm_one
    grads = (
        attend_gain_grad,
        attend_shift_grad,
        triple_weight_grad,
        query_bias_grad,
        value_bias_grad,
        merge_weight_grad,
        merge_bias_grad,
        feed_gain_grad,
        feed_shift_grad,
        up_weight_grad,
        up_bias_grad,
        down_weight_grad,
        down_bias_grad,
    )
    return (grads, grad_rows)


def on_device(
    cube_tokens,
    visible,
    padding,
    attend_gain,
    attend_shift,
    triple_weight,
    query_bias,
    value_bias,
    merge_weight,
    merge_bias,
    feed_gain,
    feed_shift,
    up_weight,
    up_bias,
    down_weight,
    down_bias,
    cotangent,
):
    slots = cube_tokens.shape[0]
    keep = padding.astype(jnp.float32)
    picked = jnp.arange(slots)[:, None]
    rows = cube_tokens[picked, visible].astype(jnp.float32)
    weights = fetch_weights(
        attend_gain,
        attend_shift,
        triple_weight,
        query_bias,
        value_bias,
        merge_weight,
        merge_bias,
        feed_gain,
        feed_shift,
        up_weight,
        up_bias,
        down_weight,
        down_bias,
    )
    output, saved = forward_pass(rows, keep, weights)
    weights_back = fetch_weights(
        attend_gain,
        attend_shift,
        triple_weight,
        query_bias,
        value_bias,
        merge_weight,
        merge_bias,
        feed_gain,
        feed_shift,
        up_weight,
        up_bias,
        down_weight,
        down_bias,
    )
    unused, saved = forward_pass(rows, keep, weights_back)
    grads, grad_rows = backward_pass(keep, weights_back, saved, cotangent)
    cube_gradient = jnp.zeros(cube_tokens.shape, jnp.float32).at[picked, visible].add(grad_rows)
    summed = reduce_gradients(grads)
    return (
        output,
        cube_gradient,
        summed[0],
        summed[1],
        summed[2],
        summed[3],
        summed[4],
        summed[5],
        summed[6],
        summed[7],
        summed[8],
        summed[9],
        summed[10],
        summed[11],
        summed[12],
    )


def solution(mesh):
    placed = (
        P(("gx", "gy"), None, None),
        P(("gx", "gy"), None),
        P(("gx", "gy"), None),
        P(("gx", "gy")),
        P(("gx", "gy")),
        P(("gx", "gy"), None),
        P(("gx", "gy")),
        P(("gx", "gy")),
        P(("gx", "gy"), None),
        P(("gx", "gy")),
        P(("gx", "gy")),
        P(("gx", "gy")),
        P(("gx", "gy"), None),
        P(("gx", "gy")),
        P(("gx", "gy"), None),
        P(("gx", "gy")),
        P(("gx", "gy"), None, None),
    )
    return jax.shard_map(
        on_device,
        mesh=mesh,
        in_specs=placed,
        out_specs=(
            P(("gx", "gy"), None, None),
            P(("gx", "gy"), None, None),
            P(("gx", "gy")),
            P(("gx", "gy")),
            P(("gx", "gy"), None),
            P(("gx", "gy")),
            P(("gx", "gy")),
            P(("gx", "gy"), None),
            P(("gx", "gy")),
            P(("gx", "gy")),
            P(("gx", "gy")),
            P(("gx", "gy"), None),
            P(("gx", "gy")),
            P(("gx", "gy"), None),
            P(("gx", "gy")),
        ),
        check_vma=False,
    )
```

profile of v0, /device:TPU:0, one launch (start us, length us, event | category | flops | bytes accessed | tf_op | source)
XLA Modules:
  0.0 833.1 jit_solution(16576735448332200841)
XLA Ops:
  8.0 0.7 all-gather.7.cloned.1.call-update
  10.0 0.7 broadcast_compare_fusion
  10.7 0.7 convert_element_type.164
  11.4 0.8 dynamic-update-slice
  12.3 0.8 dynamic-update-slice.1
  13.1 0.8 dynamic-update-slice.2
  13.9 0.8 dynamic-update-slice.3
  14.8 0.8 dynamic-update-slice.4
  15.6 0.8 dynamic-update-slice.5
  16.4 0.8 dynamic-update-slice.6
  17.3 0.8 dynamic-update-slice.8
  18.1 0.8 dynamic-update-slice.7
  18.9 43.0 %all-reduce.19 = (bf16[768]{0:T(1024)(128)(2,1)S(1)}, bf16[768]{0:T(1024)(128)(2,1)S(1)}, bf16[768]{0:T(1024)(128)(2,1)S(1)}, bf16[768]{0:T(1024)(128)(2,1)S(1)}...) all-reduce(bf16[768]{0:T(1024)(128)(2,1)S(1)} %dynamic-update-slice, ...), channel_id=1, replica_groups=mesh['gx'=4,'gy'=8] {'gx','gy'}, use_global_device_ids=true, to_apply=%add.6 | all-reduce | flops 9216 | bytes 36864
  62.0 1.3 or_select_fusion
  63.3 9.0 %gather_fusion = bf16[768,768]{1,0:T(8,128)(2,1)S(1)} fusion(bf16[2,1536,768]{2,1,0:T(8,128)(2,1)} %param.17, s32[768]{0:T(1024)S(1)} %reshape.295), kind=kCustom, calls=%fused_computation | custom fusion | bytes 2365440 | tf_op jit(solution)/shard_map/gather | solution.py:305
  72.5 1.8 multiply_reduce_fusion.6
  75.6 1.3 fusion.26
  77.0 6.7 add_convert_fusion
  83.7 5.8 copy.56
  89.4 7.9 reshape.287
  97.3 3.9 fusion.50
  101.3 7.2 fusion.22
  108.5 8.1 fusion
  116.6 7.5 fusion.31
  124.2 1.2 copy.61
  125.4 1.3 copy.79
  126.7 3.0 all-gather.7.cloned.1.call-done
  129.7 2.9 fusion.47
  134.4 1.5 log_add_fusion
  135.8 2.2 add_convert_fusion.2
  138.1 57.1 %all-gather.9.cloned.1.call-done = bf16[768,3072]{1,0:T(8,128)(2,1)} async-done(((bf16[24,3072]{1,0:T(8,128)(2,1)}), bf16[768,3072]{1,0:T(8,128)(2,1)}) %all-gather.9.cloned.1.call-update) | async-done | bytes 4718608 | tf_op jit(solution)/shard_map/all_gather | solution.py:57
  195.2 27.1 %fusion.4 = (bf16[768,3072]{1,0:T(8,128)(2,1)}, f32[768,3072]{1,0:T(8,128)}) fusion(f32[3072]{0:T(1024)} %convert_element_type.173, bf16[768,768]{1,0:T(8,128)(2,1)} %add_convert_fusion.2, bf16[768,3072]{1,0:T(8,128)(2,1)} %all-gather.9.cloned.1.call-done), kind=kOutput, calls=%fused_computation.14 | convolution fusion | flops 3779592192 | bytes 20066304 | tf_op jit(solution)/shard_map/dot_general | solution.py:139
  222.3 38.1 %all-gather.11.cloned.1.call-done = bf16[3072,768]{1,0:T(8,128)(2,1)} async-done(((bf16[96,768]{1,0:T(8,128)(2,1)}), bf16[3072,768]{1,0:T(8,128)(2,1)}) %all-gather.11.cloned.1.call-update) | async-done | bytes 4718608 | tf_op jit(solution)/shard_map/all_gather | solution.py:59
  260.4 11.4 %convert_reduce_fusion = (f32[3072]{0:T(1024)}, bf16[768,3072]{1,0:T(8,128)(2,1)S(1)}) fusion(f32[768,3072]{1,0:T(8,128)} %get-tuple-element.67, f32[3072]{0:T(1024)} %convert_element_type.173, bf16[768,768]{1,0:T(8,128)(2,1)} %bitcast.112, bf16[3072,768]{1,0:T(8,128)(2,1)} %all-gather.11.cloned.1.call-done), kind=kOutput, calls=%fused_computation.21 | convolution fusion | flops 3654546432 | bytes 20078592 | tf_op jit(solution)/shard_map/rd,fd->rf/dot_general | solution.py:199
  271.9 6.2 multiply_reduce_fusion.1
  278.7 3.9 convert_reduce_fusion.2
  282.6 2.5 fusion.53
  285.2 1.1 convolution_convert_fusion
  286.3 1.5 copy.62
  287.8 3.8 reshape.293
  291.6 15.5 %multiply_reduce_fusion = (f32[2,12,384]{2,1,0:T(8,128)S(1)}, f32[2,12,384,384]{2,3,1,0:T(8,128)}) fusion(f32[2,12,384]{2,1,0:T(8,128)S(1)} %copy-done.20, f32[2,12,384,384]{2,3,1,0:T(8,128)} %get-tuple-element.59, pred[2,384]{1,0:T(4,128)(4,1)S(1)} %broadcast_compare_fusion, bf16[2,384,1,12,64]{1,0,4,3,2:T(2,128)(2,1)S(1)} %copy-done.13, ...), kind=kOutput, calls=%fused_computation.3 | convolution fusion | flops 470670336 | bytes 30745344 | tf_op jit(solution)/shard_map/slhe,smhe->shlm/dot_general | solution.py:234
  307.2 7.5 multiply_convert_fusion
  314.7 3.0 copy-done
  317.6 1.3 multiply_bitcast_fusion.1
  319.0 5.7 multiply_bitcast_fusion
  324.7 8.5 %fusion.27 = bf16[2,384,1,12,64]{1,4,3,0,2:T(8,128)(2,1)S(1)} fusion(f32[2,12,384]{2,1,0:T(8,128)S(1)} %copy-done.21, f32[2,12,384,384]{2,3,1,0:T(8,128)} %get-tuple-element.59, pred[2,384]{1,0:T(4,128)(4,1)S(1)} %broadcast_compare_fusion, bf16[2,384,12,64]{1,0,3,2:T(2,128)(2,1)S(1)} %copy-done.14), kind=kOutput, calls=%fused_computation.70 | convolution fusion | flops 467140608 | bytes 16552704 | tf_op jit(solution)/shard_map/shlm,slhe->smhe/dot_general | solution.py:231
  333.3 1.6 convert_reduce_fusion.1
  335.5 3.6 copy.70
  339.8 1.0 copy-done.3
  340.9 1.1 copy-done.54
  342.0 5.7 multiply_reduce_fusion.2
  347.7 5.1 fusion.52
  352.8 1.2 copy-done.16
  354.1 8.9 %fusion.54 = f32[768,3072]{1,0:T(8,128)} fusion(bf16[768,768]{1,0:T(8,128)(2,1)S(1)} %copy-done.16, bf16[768,3072]{1,0:T(8,128)(2,1)} %copy-done.15), kind=kOutput, calls=%fused_computation.115 | convolution fusion | flops 3623878656 | bytes 15335424 | tf_op jit(solution)/shard_map/rd,rf->df/dot_general | solution.py:203
  363.1 1.2 copy-done.18
  364.3 9.0 %fusion.55 = f32[3072,768]{1,0:T(8,128)} fusion(bf16[768,3072]{1,0:T(8,128)(2,1)} %get-tuple-element.66, bf16[768,768]{1,0:T(8,128)(2,1)S(1)} %bitcast.113), kind=kOutput, calls=%fused_computation.116 | convolution fusion | flops 3623878656 | bytes 15335424 | tf_op jit(solution)/shard_map/rf,rd->fd/dot_general | solution.py:197
  374.3 7.3 convolution_add_fusion.1
  381.8 3.8 multiply_add_fusion
  385.6 40.7 %all-reduce.18 = (f32[768]{0:T(1024)S(1)}, f32[768]{0:T(1024)S(1)}, f32[768]{0:T(1024)S(1)}, f32[768]{0:T(1024)S(1)}, f32[768]{0:T(1024)S(1)}, /*index=5*/f32[76...) all-reduce(f32[768]{0:T(1024)S(1)} %copy-done.48, ...), channel_id=2, replica_groups=mesh['gx'=4,'gy'=8] {'gx','gy'}, use_global_device_ids=true, to_apply=%region_13.14.clone | all-reduce | flops 9216 | bytes 73728
  431.6 4.3 broadcast_in_dim.30
  435.9 102.8 %scatter_fusion = f32[2,1536,768]{2,1,0:T(8,128)} fusion(f32[2,1536,768]{2,1,0:T(8,128)} %broadcast_in_dim.30, s32[768]{0:T(1024)S(1)} %reshape.301, f32[768,768]{1,0:T(8,128)S(1)} %bitcast.103), kind=kCustom, calls=%fused_computation.1 | custom fusion | flops 589824 | bytes 7084032 | tf_op jit(solution)/shard_map/scatter-add | solution.py:339
  538.8 3.5 reduce-scatter.5.cloned.1.call-done
  542.3 141.5 %reduce-scatter.9.cloned.1.call-done = f32[24,3072]{1,0:T(8,128)} async-done(((f32[768,3072]{1,0:T(8,128)}), f32[24,3072]{1,0:T(8,128)}) %reduce-scatter.9.cloned.1.call-update) | async-done | bytes 294928 | tf_op jit(solution)/shard_map/reduce_scatter | solution.py:76
  683.7 142.1 %reduce-scatter.11.cloned.1.call-done = f32[96,768]{1,0:T(8,128)} async-done(((f32[3072,768]{1,0:T(8,128)}), f32[96,768]{1,0:T(8,128)}) %reduce-scatter.11.cloned.1.call-update) | async-done | bytes 294928 | tf_op jit(solution)/shard_map/reduce_scatter | solution.py:78
  (184 shorter events, 13.7 us)
Async XLA Ops:
  7.2 69.7 %all-gather.5.cloned.1.call-start = ((), (), s32[]{:S(2)}) async-start(), calls=%async_computation.4 | async-start | bytes 3649536 | tf_op jit(solution)/shard_map/all_gather | solution.py:50
  7.9 121.8 %all-gather.7.cloned.1.call-start = ((), (), s32[]{:S(2)}) async-start(), calls=%async_computation.5 | async-start | bytes 1216512 | tf_op jit(solution)/shard_map/all_gather | solution.py:53
  8.7 186.5 %all-gather.9.cloned.1.call-start = ((), (), s32[]{:S(2)}) async-start(), calls=%async_computation.6 | async-start | bytes 4866048 | tf_op jit(solution)/shard_map/all_gather | solution.py:57
  9.4 251.0 %all-gather.11.cloned.1.call-start = ((), (), s32[]{:S(2)}) async-start(), calls=%async_computation.7 | async-start | bytes 4866048 | tf_op jit(solution)/shard_map/all_gather | solution.py:59
  10.0 528.8 %reduce-scatter.7.cloned.1.call-start = ((), (), s32[]{:S(2)}) async-start(), calls=%async_computation.9 | async-start | bytes 2433024 | tf_op jit(solution)/shard_map/reduce_scatter | solution.py:72
  11.4 64.2 %copy-start.25 = (f32[2,384]{1,0:T(2,128)}, f32[2,384]{1,0:T(2,128)S(1)}, u32[]{:S(2)}) copy-start(f32[2,384]{1,0:T(2,128)S(1)} %convert_element_type.164) | copy-start | bytes 9220
  62.0 15.0 %copy-start.39 = (f32[768]{0:T(1024)}, f32[768]{0:T(1024)S(1)}, u32[]{:S(2)}) copy-start(f32[768]{0:T(1024)S(1)} %convert_element_type.158) | copy-start | bytes 9220
  62.0 15.0 %copy-start.44 = (f32[768]{0:T(1024)}, f32[768]{0:T(1024)S(1)}, u32[]{:S(2)}) copy-start(f32[768]{0:T(1024)S(1)} %convert_element_type.159) | copy-start | bytes 9220
  72.3 3.3 copy-start.4
  72.5 1.8 copy-start.35
  74.3 9.3 %copy-start.32 = (f32[2,384]{1,0:T(2,128)}, f32[2,384]{1,0:T(2,128)S(1)}, u32[]{:S(2)}) copy-start(f32[2,384]{1,0:T(2,128)S(1)} %add_rsqrt_fusion.1) | copy-start | bytes 9220
  101.2 7.2 copy-start.6
  101.2 7.2 copy-start.8
  101.3 15.4 %copy-start.12 = (bf16[2,384,1,12,64]{1,0,4,3,2:T(2,128)(2,1)}, bf16[2,384,1,12,64]{1,0,4,3,2:T(2,128)(2,1)S(1)}, u32[]{:S(2)}) copy-start(bf16[2,384,1,12,64]{1,0,4,3,2:T(2,128)(2,1)S(1)} %get-tuple-element.49) | copy-start | bytes 3538948
  108.5 8.1 copy-start.22
  116.6 7.6 copy-start.23
  132.6 146.1 %copy-start.1 = (f32[768,768]{1,0:T(8,128)}, f32[768,768]{1,0:T(8,128)S(1)}, u32[]{:S(2)}) copy-start(f32[768,768]{1,0:T(8,128)S(1)} %get-tuple-element.61) | copy-start | bytes 7077892
  133.8 88.5 %copy-start.27 = (f32[768]{0:T(1024)}, f32[768]{0:T(1024)S(1)}, u32[]{:S(2)}) copy-start(f32[768]{0:T(1024)S(1)} %add_rsqrt_fusion) | copy-start | bytes 9220
  260.4 11.4 %copy-start.28 = (f32[768]{0:T(1024)S(1)}, f32[768]{0:T(1024)}, u32[]{:S(2)}) copy-start(f32[768]{0:T(1024)} %copy-done.27) | copy-start | bytes 9220
  260.4 11.4 %copy-start.53 = (bf16[768,3072]{1,0:T(8,128)(2,1)S(1)}, bf16[768,3072]{1,0:T(8,128)(2,1)}, u32[]{:S(2)}) copy-start(bf16[768,3072]{1,0:T(8,128)(2,1)} %all-gather.9.cloned.1.call-done) | copy-start | bytes 14155780
  271.8 6.2 copy-start.15
  271.9 6.8 copy-start.26
  278.7 3.9 copy-start.19
  282.6 2.5 copy-start.55
  286.3 5.3 copy-start.13
  286.3 5.3 copy-start.20
  287.8 19.4 %slice-start = ((s8[14155776]{0:T(1024)(128)(4,1)}), s8[1572864]{0:T(1024)(128)(4,1)S(1)}, s32[]{:S(2)}) async-start(s8[14155776]{0:T(1024)(128)(4,1)} %bitcast.97), calls=%async_computation.12 | async-start | bytes 3145728
  291.6 15.6 %slice-start.1 = ((s8[14155776]{0:T(1024)(128)(4,1)}), s8[4194304]{0:T(1024)(128)(4,1)S(1)}, s32[]{:S(2)}) async-start(s8[14155776]{0:T(1024)(128)(4,1)} %bitcast.97), calls=%async_computation.13 | async-start | bytes 8388608
  291.6 15.6 %slice-start.2 = ((s8[14155776]{0:T(1024)(128)(4,1)}), s8[4194304]{0:T(1024)(128)(4,1)S(1)}, s32[]{:S(2)}) async-start(s8[14155776]{0:T(1024)(128)(4,1)} %bitcast.97), calls=%async_computation.14 | async-start | bytes 8388608
  291.6 15.6 %slice-start.3 = ((s8[14155776]{0:T(1024)(128)(4,1)}), s8[4194304]{0:T(1024)(128)(4,1)S(1)}, s32[]{:S(2)}) async-start(s8[14155776]{0:T(1024)(128)(4,1)} %bitcast.97), calls=%async_computation.15 | async-start | bytes 8388608
  307.2 10.4 %copy-start.9 = (bf16[2,384,1,12,64]{1,0,4,3,2:T(2,128)(2,1)S(1)}, bf16[2,384,1,12,64]{1,0,4,3,2:T(2,128)(2,1)}, u32[]{:S(2)}) copy-start(bf16[2,384,1,12,64]{1,0,4,3,2:T(2,128)(2,1)} %copy-done.8) | copy-start | bytes 3538948
  314.6 3.0 copy-start
  317.6 1.4 copy-start.7
  318.9 5.8 copy-start.14
  319.0 223.3 %reduce-scatter.5.cloned.1.call-start = ((), (), s32[]{:S(2)}) async-start(), calls=%async_computation.8 | async-start | bytes 7299072 | tf_op jit(solution)/shard_map/reduce_scatter | solution.py:69
  319.0 5.7 copy-start.21
  339.2 1.7 copy-start.3
  339.2 1.7 copy-start.33
  339.2 1.7 copy-start.36
  339.2 1.7 copy-start.40
  339.2 1.7 copy-start.45
  339.2 2.8 copy-start.54
  352.8 1.3 copy-start.16
  352.8 331.0 %reduce-scatter.9.cloned.1.call-start = ((), (), s32[]{:S(2)}) async-start(), calls=%async_computation.10 | async-start | bytes 9732096 | tf_op jit(solution)/shard_map/reduce_scatter | solution.py:76
  363.0 1.3 copy-start.18
  363.0 462.8 %reduce-scatter.11.cloned.1.call-start = ((), (), s32[]{:S(2)}) async-start(), calls=%async_computation.11 | async-start | bytes 9732096 | tf_op jit(solution)/shard_map/reduce_scatter | solution.py:78
  373.3 0.9 copy-start.50
  374.2 7.4 copy-start.2
  374.2 7.4 copy-start.5
  374.2 7.4 copy-start.11
  374.2 7.4 copy-start.17
  374.3 7.4 copy-start.29
  374.3 7.4 copy-start.30
  374.3 7.4 copy-start.31
  374.3 7.4 copy-start.34
  374.3 7.4 copy-start.37
  374.3 7.4 copy-start.41
  381.7 3.8 copy-start.38
  381.7 3.8 copy-start.43
  381.8 3.8 copy-start.46
  381.8 3.8 copy-start.47
  381.8 3.8 copy-start.48
  381.8 3.8 copy-start.49
  431.6 4.4 copy-start.10
  (4 other events, 3.0 us)
Sparse Core Ops, SparseCore 0:
  10.9 63.2 all-gather.4
  77.1 52.5 all-gather.6
  132.6 62.5 all-gather.8
  198.0 62.4 all-gather.10
  319.1 97.8 reduce-scatter.6
  424.0 118.2 reduce-scatter.4
  548.8 134.9 reduce-scatter.8
  691.2 134.5 reduce-scatter.10
where the time goes:
time: 847 us; the launch traced here: 833 us
  waiting for transfers between devices  388 us (46%)
  matrix products  140 us (17%)
  other arithmetic  139 us (16%)
  blocking collectives  83.7 us (10%)
  local copies, waits for them, and re-layouts  66.7 us (8%)
  between operations  15.4 us (2%)
    reduce_scatter x1, waiting for transfers between devices, reduce_gradients(): lax.psum_scatter(grads[11], ('gx', 'gy'), scatter_dimension=0, tiled=True)  142 us
    reduce_scatter x1, waiting for transfers between devices, reduce_gradients(): lax.psum_scatter(grads[9], ('gx', 'gy'), scatter_dimension=0, tiled=True)  141 us
    scatter-add x1, other arithmetic, on_device(): jnp.zeros(cube_tokens.shape, jnp.float32).at[picked, visible].add(grad_rows)  103 us
    unnamed x2, blocking collectives  83.7 us
    all_gather x1, waiting for transfers between devices, fetch_weights(): lax.all_gather(up_weight, ('gx', 'gy'), axis=0, tiled=True)  57.1 us
    all_gather x1, waiting for transfers between devices, fetch_weights(): lax.all_gather(down_weight, ('gx', 'gy'), axis=0, tiled=True)  38.1 us
    dot_general x1, matrix products, forward_pass(): jnp.dot(second_low, up_weight, preferred_element_type=jnp.float32)  27.1 us
    unnamed x149, local copies, waits for them, and re-layouts  23.1 us
  transfers between devices with their start and end apart: 8, of which 6 were waited for; matrix products, arithmetic and copies ran while one was open for 34% of the time, Pallas kernels for 0%

commit v1 on v0

v1 whole, which is shorter than its diff:
```python
import functools

import jax
import jax.numpy as jnp
from jax import lax
from jax.experimental import pallas as pl
from jax.experimental.pallas import tpu as pltpu
from jax.sharding import PartitionSpec as P

HEADS = 12
HEAD = 64
PAIR = 2 * HEAD
LANES = 128
QUARTERS = 4
VECS = 16
EPS = 1e-06
BOTH = ("gx", "gy")
BF = jnp.bfloat16
F32 = jnp.float32
MEGA = 1 << 20
(
    ATTEND_GAIN,
    ATTEND_SHIFT,
    QUERY_BIAS,
    VALUE_BIAS,
    MERGE_BIAS,
    FEED_GAIN,
    FEED_SHIFT,
    DOWN_BIAS,
    UP_BIAS,
) = range(9)


class Plan:
    def __init__(self, mesh):
        self.depth = mesh.shape["gx"]
        self.inner = mesh.shape["gy"]
        self.bits = (self.inner // 2).bit_length() - 1
        assert self.inner == 2 << self.bits
        self.pieces = 1 << self.bits
        self.chips = self.depth * self.pieces

    def position(self):
        z = lax.axis_index("gx")
        gy = lax.axis_index("gy")
        return z, gy // 2, gy % 2

    def bit(self, core, place):
        return self.bits - 1 - place if core == 0 else place

    def mask(self, core, piece):
        return sum(1 << self.bit(core, p) for p in range(self.bits) if piece >> p & 1)

    def table(self):
        z, plane, core = self.position()
        rows = []
        for sibling in (0, 1):
            for piece in range(self.pieces):
                at = core ^ sibling
                flip = jnp.where(at == 0, self.mask(0, piece), self.mask(1, piece))
                for shift in range(self.depth):
                    rows.append((z - shift) % self.depth * self.pieces + (plane ^ flip))
        return jnp.stack([jnp.asarray(r, jnp.int32) for r in rows] + [core.astype(jnp.int32)])

    def swap_core(self, x):
        pairs = [(i, i ^ 1) for i in range(self.depth * self.inner)]
        return lax.ppermute(x, BOTH, pairs)

    def swap_place(self, x, place):
        pairs = []
        for i in range(self.depth * self.inner):
            core = i & 1
            pairs.append((i, i ^ (2 << self.bit(core, place))))
        return lax.ppermute(x, BOTH, pairs)

    def shift(self, x, by):
        count = self.depth * self.inner
        pairs = [(i, (i + by * self.inner) % count) for i in range(count)]
        return lax.ppermute(x, BOTH, pairs)


def chip_block(plan, shard, cuts):
    rows, width = shard.shape
    half = width // 2
    _, _, core = plan.position()
    kept = lax.dynamic_slice(shard, (0, core * half), (rows, half))
    sent = lax.dynamic_slice(shard, (0, (1 - core) * half), (rows, half))
    got = plan.swap_core(sent)
    block = jnp.where(
        core == 0,
        jnp.concatenate([kept, got], axis=0),
        jnp.concatenate([got, kept], axis=0),
    )
    return [block[:, a:b] for a, b in zip((0,) + cuts, cuts + (half,))]


class Gather:
    def __init__(self, plan):
        self.plan = plan
        self.own, self.other = {}, {}

    @staticmethod
    def column(plan, block, cuts, *before):
        block = tie(block, *before)
        column = [block] + [plan.shift(block, k) for k in range(1, plan.depth)]
        out = []
        for a, b in zip((0,) + cuts, cuts + (block.shape[1],)):
            group = Gather(plan)
            group.own[0] = jnp.stack([x[:, a:b] for x in column])
            out.append(group)
        return out

    def hold(self, *before):
        self.own[0] = tie(self.own[0], *before)

    def meet(self, stage, *before):
        for piece in range(1, self.plan.pieces):
            if bin(piece).count("1") == stage + 1:
                place = piece.bit_length() - 1
                near = tie(self.own[piece ^ (1 << place)], *before)
                self.own[piece] = self.plan.swap_place(near, place)

    def share(self, stage, *before):
        for piece in range(self.plan.pieces):
            if bin(piece).count("1") == stage:
                self.other[piece] = self.plan.swap_core(tie(self.own[piece], *before))

    def pieces(self):
        order = range(self.plan.pieces)
        return [self.own[p] for p in order], [self.other[p] for p in order]


class Scatter:
    def __init__(self, plan, mine, theirs):
        self.plan = plan
        self.size = mine.shape[0]
        self.rows = mine.shape[1] // 2
        self.parts = [mine, plan.swap_core(theirs)]
        self.place = plan.bits

    def total(self, low, high, parts=None):
        parts = self.parts if parts is None else parts
        out = parts[0][low:high].astype(F32)
        for part in parts[1:]:
            out = out + part[low:high].astype(F32)
        return out

    def meet(self, *before):
        self.place -= 1
        self.size //= 2
        send = self.total(self.size, 2 * self.size).astype(BF)
        self.sent = tie(send, *before)
        self.parts.append(self.plan.swap_place(self.sent, self.place))

    def column(self, *before):
        sends = [self.total(k, k + 1).astype(BF) for k in range(1, self.plan.depth)]
        sends = tie(tuple(sends), *before)
        self.sent = sends[-1]
        self.parts.extend([self.plan.shift(x, -1 - k) for k, x in enumerate(sends)])

    def finish(self):
        _, _, core = self.plan.position()
        done = self.total(0, 1)[0]
        top, bottom = done[: self.rows], done[self.rows :]
        keep = jnp.where(core == 0, top, bottom)
        got = self.plan.swap_core(jnp.where(core == 0, bottom, top))
        return jnp.where(
            core == 0,
            jnp.concatenate([keep, got], axis=1),
            jnp.concatenate([got, keep], axis=1),
        )


def tie(value, *before):
    if not before:
        return value
    return lax.optimization_barrier((value, before))[0]


def dot(a, b, dims=((1,), (0,))):
    return lax.dot_general(a, b, (dims, ((), ())), preferred_element_type=F32)


def dot_nt(a, b):
    return dot(a, b, ((1,), (1,)))


def dot_tn(a, b):
    return dot(a, b, ((0,), (0,)))


def normalize(values):
    center = values - jnp.mean(values, axis=-1, keepdims=True)
    scale = lax.rsqrt(jnp.mean(center * center, axis=-1, keepdims=True) + EPS)
    return center * scale, scale


def normalize_back(grad, normed, scale, gain):
    inner = grad * gain
    mean = jnp.mean(inner, axis=-1, keepdims=True)
    along = jnp.mean(inner * normed, axis=-1, keepdims=True)
    return scale * (inner - mean - normed * along)


def gelu_parts(u):
    gauss = jnp.exp(-0.5 * u * u)
    t = 1.0 / (1.0 + (0.3275911 * 0.7071067811865476) * jnp.abs(u))
    poly = 1.061405429 * t - 1.453152027
    poly = poly * t + 1.421413741
    poly = poly * t - 0.284496736
    poly = poly * t + 0.254829592
    tail = 0.5 * poly * t * gauss
    cdf = jnp.where(u >= 0, 1.0 - tail, tail)
    return cdf, gauss * 0.3989422804014327


def copies_in(table, own, other, whole, sem, at, wide):
    count = len(own)
    depth, pair, _ = own[0].shape
    core = table[2 * count * depth]
    out = []
    for side, pieces in enumerate((own, other)):
        column = pl.multiple_of((core if side == 0 else 1 - core) * wide, LANES)
        for p, piece in enumerate(pieces):
            for k in range(depth):
                chip = table[(side * count + p) * depth + k]
                row = pl.multiple_of(chip * pair, 16)
                out.append(
                    pltpu.make_async_copy(
                        piece.at[k, :, pl.ds(at, wide)],
                        whole.at[pl.ds(row, pair), pl.ds(column, wide)],
                        sem,
                    )
                )
    return out


def copies_out(table, whole, mine, theirs, sem, count, depth, at, wide):
    pair = mine.shape[1]
    core = table[2 * count * depth]
    out = []
    for side, blocks in enumerate((mine, theirs)):
        column = pl.multiple_of((core if side == 0 else 1 - core) * wide, LANES)
        for b in range(count * depth):
            chip = table[side * count * depth + b]
            row = pl.multiple_of(chip * pair, 16)
            out.append(
                pltpu.make_async_copy(
                    whole.at[pl.ds(row, pair), pl.ds(column, wide)],
                    blocks.at[b, :, pl.ds(at, wide)],
                    sem,
                )
            )
    return out


ANY = pl.BlockSpec(memory_space=pl.ANY)
SMEM = pl.BlockSpec(memory_space=pltpu.SMEM)
VMEM = pl.BlockSpec(memory_space=pltpu.VMEM)


def far(shape, dtype):
    return pltpu.HBM(shape, dtype)


def params(mebibytes, **more):
    return pltpu.CompilerParams(vmem_limit_bytes=mebibytes * MEGA, **more)


def pack_kernel(triple_ref, vec_ref, out_ref):
    share, wide = triple_ref.shape
    count = vec_ref.shape[0]
    out_ref[:, :wide] = triple_ref[...]
    vecs = vec_ref[...].astype(F32)
    vecs = jnp.concatenate([vecs, jnp.zeros((LANES - count, share), F32)], axis=0)
    vecs = jnp.concatenate([vecs, jnp.zeros((LANES, LANES - share), F32)], axis=1)
    out_ref[:, wide : wide + LANES] = vecs.T[:share].astype(BF)
    out_ref[:, wide + LANES :] = jnp.zeros((share, LANES), BF)


def pack(triple, vectors):
    share, wide = triple.shape
    return pl.pallas_call(
        pack_kernel,
        in_specs=[VMEM] * 2,
        out_specs=VMEM,
        out_shape=jax.ShapeDtypeStruct((share, wide + 2 * LANES), BF),
        compiler_params=params(16),
        name="pack",
    )(triple, vectors)


def part_kernel(up_ref, down_ref, merge_ref, out_ref, wide_up):
    share, width = merge_ref.shape
    devices = width // share
    half = out_ref.shape[1] // 2
    wide_up[...] = up_ref[...].astype(F32)
    starts = [0] + [width * j + width // 2 for j in range(1, QUARTERS)]
    for j, start in enumerate(starts):
        for group in range(0, width, LANES):
            lanes = []
            column = group
            while column < group + LANES:
                device, inside = divmod(column, share)
                count = min(share - inside, group + LANES - column)
                at = device * QUARTERS * share + j * share + inside
                lanes.append(wide_up[:, at : at + count])
                column += count
            out_ref[:, start + group : start + group + LANES] = jnp.concatenate(lanes, axis=1).astype(BF)
        out_ref[:, half + start : half + start + width] = down_ref[j * share : (j + 1) * share]
    for side in range(2):
        at = side * half + width
        out_ref[:, at : at + width // 2] = merge_ref[:, side * width // 2 : (side + 1) * width // 2]


def part(up, down, merge):
    share, width = merge.shape
    return pl.pallas_call(
        part_kernel,
        in_specs=[VMEM] * 3,
        out_specs=VMEM,
        out_shape=jax.ShapeDtypeStruct((share, 9 * width), BF),
        scratch_shapes=[pltpu.VMEM((share, QUARTERS * width), F32)],
        compiler_params=params(16),
        name="part",
    )(up, down, merge)


def weave_kernel(early_ref, later_ref, up_ref, down_ref):
    share, wide = early_ref.shape
    width = wide // QUARTERS
    devices = width // share
    for group in range(0, QUARTERS * width, LANES):
        lanes = []
        column = group
        while column < group + LANES:
            device, rest = divmod(column, QUARTERS * share)
            j, inside = divmod(rest, share)
            count = min(share - inside, group + LANES - column)
            source = early_ref if j < 2 else later_ref
            at = (j % 2) * width + device * share + inside
            lanes.append(source[:, at : at + count])
            column += count
        up_ref[:, group : group + LANES] = jnp.concatenate(lanes, axis=1)
    for j in range(QUARTERS):
        source = early_ref if j < 2 else later_ref
        at = (2 + j % 2) * width
        down_ref[j * share : (j + 1) * share] = source[:, at : at + width]


def weave(early, later):
    share, wide = early.shape
    return pl.pallas_call(
        weave_kernel,
        in_specs=[VMEM] * 2,
        out_specs=[VMEM] * 2,
        out_shape=[
            jax.ShapeDtypeStruct((share, wide), F32),
            jax.ShapeDtypeStruct((QUARTERS * share, wide // QUARTERS), F32),
        ],
        compiler_params=params(16),
        name="weave",
    )(early, later)


def pick_kernel(cube_ref, seen_ref, rows_ref):
    tokens = cube_ref.shape[1]
    length = rows_ref.shape[0]
    at = lax.broadcasted_iota(jnp.int32, (length, tokens), 1)
    hot = jnp.where(at == seen_ref[0], 1.0, 0.0).astype(BF)
    rows_ref[...] = dot(hot, cube_ref[0]).astype(BF)


def pick_rows(cube, seen):
    slots, tokens, width = cube.shape
    length = seen.shape[1]
    return pl.pallas_call(
        pick_kernel,
        grid=(slots,),
        in_specs=[
            pl.BlockSpec((1, tokens, width), lambda s: (s, 0, 0)),
            pl.BlockSpec((1, length, 1), lambda s: (s, 0, 0)),
        ],
        out_specs=pl.BlockSpec((length, width), lambda s: (s, 0)),
        out_shape=jax.ShapeDtypeStruct((slots * length, width), BF),
        compiler_params=params(48),
        name="pick",
    )(cube, seen.reshape(slots, length, 1))


def spread_kernel(seen_ref, high_ref, low_ref, out_ref):
    block, length = out_ref.shape[1], high_ref.shape[0]
    base = pl.program_id(1) * block
    at = base + lax.broadcasted_iota(jnp.int32, (block, length), 0)
    hot = jnp.where(at == seen_ref[0], 1.0, 0.0).astype(BF)
    out_ref[0] = dot(hot, high_ref[...]) + dot(hot, low_ref[...])


def spread_rows(seen, high, low, tokens):
    slots, length = seen.shape
    width = high.shape[1]
    block = tokens // 2
    return pl.pallas_call(
        spread_kernel,
        grid=(slots, tokens // block),
        in_specs=[
            pl.BlockSpec((1, 1, length), lambda s, t: (s, 0, 0)),
            pl.BlockSpec((length, width), lambda s, t: (s, 0)),
            pl.BlockSpec((length, width), lambda s, t: (s, 0)),
        ],
        out_specs=pl.BlockSpec((1, block, width), lambda s, t: (s, t, 0)),
        out_shape=jax.ShapeDtypeStruct((slots, tokens, width), F32),
        compiler_params=params(48),
        name="spread",
    )(seen.reshape(slots, 1, length), high, low)


def triple_kernel(pieces, table, rows_ref, *refs):
    own, other = refs[:pieces], refs[pieces : 2 * pieces]
    first_ref, triple_ref, weight_ref, vec_ref, whole, sem, sem_out = refs[2 * pieces :]
    width = rows_ref.shape[1]
    moves = copies_in(table, own, other, whole, sem, 0, own[0].shape[2])
    for move in moves:
        move.start()
    normed, _ = normalize(rows_ref[...].astype(F32))
    for move in moves:
        move.wait()
    keep = pltpu.make_async_copy(whole.at[:, pl.ds(0, 3 * width)], weight_ref, sem_out)
    keep.start()
    vecs = whole[:, 3 * width : 3 * width + LANES].astype(F32).T[:VECS]
    vec_ref[...] = vecs
    first = normed * vecs[ATTEND_GAIN : ATTEND_GAIN + 1] + vecs[ATTEND_SHIFT : ATTEND_SHIFT + 1]
    first = first.astype(BF)
    first_ref[...] = first
    for part, bias in enumerate((QUERY_BIAS, None, VALUE_BIAS)):
        cols = slice(part * width, (part + 1) * width)
        out = dot(first, whole[:, cols])
        if bias is not None:
            out = out + vecs[bias : bias + 1]
        triple_ref[:, cols] = out.astype(BF)
    keep.wait()


def project(plan, table, rows, own, other):
    count, width = rows.shape
    pieces = len(own)
    half = own[0].shape[2]
    return pl.pallas_call(
        functools.partial(triple_kernel, pieces),
        in_specs=[SMEM, VMEM] + [ANY] * (2 * pieces),
        out_specs=[VMEM, VMEM, ANY, VMEM],
        out_shape=[
            far((count, width), BF),
            far((count, 3 * width), BF),
            far((width, 3 * width), BF),
            jax.ShapeDtypeStruct((VECS, width), F32),
        ],
        scratch_shapes=[
            pltpu.VMEM((width, 2 * half), BF),
            pltpu.SemaphoreType.DMA,
            pltpu.SemaphoreType.DMA,
        ],
        compiler_params=params(32),
        name="project",
    )(table, rows, *own, *other)


def attend_kernel(q_ref, k_ref, v_ref, keep_ref, mixed_ref, probs_ref):
    q, k, v = q_ref[...], k_ref[...], v_ref[...]
    left = lax.broadcasted_iota(jnp.int32, q.shape, 1) < HEAD
    none = jnp.zeros_like(q)
    keep = keep_ref[0] > 0
    outs = []
    for t in range(2):
        part = jnp.where(left, q, none) if t == 0 else jnp.where(left, none, q)
        scores = jnp.where(keep, dot_nt(part, k) * 0.125, -1000000000.0)
        expo = jnp.exp(scores - jnp.max(scores, axis=-1, keepdims=True))
        probs = expo * (1.0 / jnp.sum(expo, axis=-1, keepdims=True))
        probs = probs.astype(BF)
        probs_ref[0, t] = probs
        outs.append(dot(probs, v))
    mixed_ref[...] = jnp.where(left, outs[0], outs[1]).astype(BF)


def attend(triple, keep_row, part):
    slots, _, length = keep_row.shape
    count, width = triple.shape[0], triple.shape[1] // 3
    pairs = width // PAIR
    some = pairs // 2
    first = part * some
    return pl.pallas_call(
        attend_kernel,
        grid=(slots, some),
        in_specs=[
            pl.BlockSpec((length, PAIR), lambda s, g: (s, first + g)),
            pl.BlockSpec((length, PAIR), lambda s, g: (s, first + pairs + g)),
            pl.BlockSpec((length, PAIR), lambda s, g: (s, first + 2 * pairs + g)),
            pl.BlockSpec((1, 1, length), lambda s, g: (s, 0, 0)),
        ],
        out_specs=[
            pl.BlockSpec((length, PAIR), lambda s, g: (s, g)),
            pl.BlockSpec((1, 2, length, length), lambda s, g: (s * some + g, 0, 0, 0)),
        ],
        out_shape=[
            jax.ShapeDtypeStruct((count, width // 2), BF),
            far((slots * some, 2, length, length), BF),
        ],
        compiler_params=params(24),
        name="attend",
    )(triple, triple, triple, keep_row)


def attend_back_kernel(q_ref, k_ref, v_ref, probs_ref, out_ref, grad_ref, dq_ref, dk_ref, dv_ref):
    q, k, v, grad = q_ref[...], k_ref[...], v_ref[...], grad_ref[...]
    left = lax.broadcasted_iota(jnp.int32, q.shape, 1) < HEAD
    none = jnp.zeros_like(q)
    product = grad.astype(F32) * out_ref[...].astype(F32)
    dqs, dks, dvs = [], [], []
    for t in range(2):
        part = jnp.where(left, grad, none) if t == 0 else jnp.where(left, none, grad)
        inside = jnp.where(left, product, 0.0) if t == 0 else jnp.where(left, 0.0, product)
        delta = jnp.sum(inside, axis=-1, keepdims=True)
        probs = probs_ref[0, t]
        scores = (probs.astype(F32) * (dot_nt(part, v) - delta)).astype(BF)
        dvs.append(dot_tn(probs, grad))
        dqs.append(dot(scores, k))
        dks.append(dot_tn(scores, q))
    dq_ref[...] = (jnp.where(left, dqs[0], dqs[1]) * 0.125).astype(BF)
    dk_ref[...] = (jnp.where(left, dks[0], dks[1]) * 0.125).astype(BF)
    dv_ref[...] = jnp.where(left, dvs[0], dvs[1]).astype(BF)


def attend_back(triple, probs, mixed, grad, part):
    steps, _, length, _ = probs.shape
    count, width = triple.shape[0], triple.shape[1] // 3
    pairs = width // PAIR
    some = pairs // 2
    first = part * some
    column = pl.BlockSpec((length, PAIR), lambda s, g: (s, g))
    shape = jax.ShapeDtypeStruct((count, width // 2), BF)
    return pl.pallas_call(
        attend_back_kernel,
        grid=(steps // some, some),
        in_specs=[
            pl.BlockSpec((length, PAIR), lambda s, g: (s, first + g)),
            pl.BlockSpec((length, PAIR), lambda s, g: (s, first + pairs + g)),
            pl.BlockSpec((length, PAIR), lambda s, g: (s, first + 2 * pairs + g)),
            pl.BlockSpec((1, 2, length, length), lambda s, g: (s * some + g, 0, 0, 0)),
            column,
            pl.BlockSpec((length, PAIR), lambda s, g: (s, first + g)),
        ],
        out_specs=[column] * 3,
        out_shape=[shape] * 3,
        compiler_params=params(24),
        name="attend_back",
    )(triple, triple, triple, probs, mixed, grad)


def merge_kernel(pieces, at, table, rows_ref, mixed0, mixed1, cot_ref, keep_ref, vec_ref, *refs):
    own, other = refs[:pieces], refs[pieces : 2 * pieces]
    middle_ref, second_ref, low_ref, merge_ref, sem = refs[2 * pieces :]
    count, width = rows_ref.shape
    moves = copies_in(table, own, other, merge_ref, sem, at, width // 2)
    for move in moves:
        move.start()
    low_ref[...] = (cot_ref[...].astype(F32) * keep_ref[...]).astype(BF)
    vecs = vec_ref[...]
    for move in moves:
        move.wait()
    step = 256 if count % 256 == 0 else count
    for m in range(0, count, step):
        rows = slice(m, m + step)
        branch = dot(mixed0[rows], merge_ref[: width // 2]) + dot(mixed1[rows], merge_ref[width // 2 :])
        middle = rows_ref[rows].astype(F32) + (branch + vecs[MERGE_BIAS : MERGE_BIAS + 1])
        middle_ref[rows] = middle
        normed, _ = normalize(middle)
        second_ref[rows] = (
            normed * vecs[FEED_GAIN : FEED_GAIN + 1] + vecs[FEED_SHIFT : FEED_SHIFT + 1]
        ).astype(BF)


def merge(table, at, rows, mixed, cot, keep_column, vecs, own, other):
    count, width = rows.shape
    pieces = len(own)
    slim = jax.ShapeDtypeStruct((count, width), BF)
    return pl.pallas_call(
        functools.partial(merge_kernel, pieces, at),
        in_specs=[SMEM] + [VMEM] * 6 + [ANY] * (2 * pieces),
        out_specs=[VMEM] * 4,
        out_shape=[
            far((count, width), F32),
            slim,
            slim,
            far((width, width), BF),
        ],
        scratch_shapes=[pltpu.SemaphoreType.DMA],
        compiler_params=params(28),
        name="merge",
    )(table, rows, *mixed, cot, keep_column, vecs, *own, *other)


def feed_kernel(pieces, depth, quarter, at, to, fresh, table, second, low, vec_ref, *refs):
    own, other = refs[:pieces], refs[pieces : 2 * pieces]
    refs = refs[2 * pieces :]
    if quarter:
        branch_in, back_in = refs[:2]
        refs = refs[2:]
    if not fresh:
        refs = refs[2:]
    branch, back, mine, theirs, sums_ref, whole, grad, active, hidden, sem, sem_out = refs
    count, width = second.shape
    moves = copies_in(table, own, other, whole, sem, at * width, width)
    for move in moves:
        move.start()
    bias = vec_ref[UP_BIAS + quarter : UP_BIAS + quarter + 1]
    for move in moves:
        move.wait()
    up, down = whole[:, :width], whole[:, width:]
    step = 256 if count % 256 == 0 else count
    column = None
    for m in range(0, count, step):
        rows = slice(m, m + step)
        u = dot(second[rows], up) + bias
        cdf, density = gelu_parts(u)
        act = (u * cdf).astype(BF)
        active[rows] = act
        slope = (dot_nt(low[rows], down) * (cdf + u * density)).astype(BF)
        hidden[rows] = slope
        total = jnp.sum(slope.astype(F32), axis=0, keepdims=True)
        column = total if column is None else column + total
        forward, backward = dot(act, down), dot_nt(slope, up)
        branch[rows] = branch_in[rows] + forward if quarter else forward
        back[rows] = back_in[rows] + backward if quarter else backward
    grad[:, :width] = dot_tn(second[...], hidden[...]).astype(BF)
    grad[:, width:] = dot_tn(active[...], low[...]).astype(BF)
    moves = copies_out(table, grad, mine, theirs, sem_out, pieces, depth, to * width, width)
    for move in moves:
        move.start()
    sums_ref[...] = jnp.concatenate([column, jnp.zeros((7, width), F32)], axis=0)
    for move in moves:
        move.wait()


def feed(table, quarter, at, to, second, low, vecs, carried, blocks, own, other, span):
    count, width = second.shape
    pieces = len(own)
    depth, pair, _ = own[0].shape
    shape = far((pieces * depth, pair, span * width), BF)
    wide = jax.ShapeDtypeStruct((count, width), F32)
    fixed = 4 + 2 * pieces
    aliases = {fixed + i: i for i in range(len(carried))}
    aliases.update({fixed + len(carried) + i: 2 + i for i in range(len(blocks))})
    return pl.pallas_call(
        functools.partial(feed_kernel, pieces, depth, quarter, at, to, not blocks),
        in_specs=[SMEM] + [VMEM] * 3 + [ANY] * (2 * pieces) + [VMEM] * len(carried) + [ANY] * len(blocks),
        out_specs=[VMEM] * 2 + [ANY] * 2 + [VMEM],
        out_shape=[wide, wide, shape, shape, jax.ShapeDtypeStruct((8, width), F32)],
        scratch_shapes=[
            pltpu.VMEM((width, 2 * width), BF),
            pltpu.VMEM((width, 2 * width), BF),
            pltpu.VMEM((count, width), BF),
            pltpu.VMEM((count, width), BF),
            pltpu.SemaphoreType.DMA,
            pltpu.SemaphoreType.DMA,
        ],
        input_output_aliases=aliases,
        compiler_params=params(32),
        name="feed",
    )(table, second, low, vecs, *own, *other, *carried, *blocks)


def turn_kernel(
    middle_ref,
    branch_ref,
    back_ref,
    low_ref,
    keep_ref,
    vec_ref,
    mixed0,
    mixed1,
    merge_ref,
    out_ref,
    grad_middle_ref,
    merge_grad_ref,
    grad_mixed_ref,
    sums_ref,
):
    width = middle_ref.shape[1]
    vecs = vec_ref[...]
    middle = middle_ref[...]
    out_ref[...] = (middle + branch_ref[...] + vecs[DOWN_BIAS : DOWN_BIAS + 1]) * keep_ref[...]
    normed, scale = normalize(middle)
    grad_second = back_ref[...]
    gain = jnp.sum(grad_second * normed, axis=0, keepdims=True)
    shift = jnp.sum(grad_second, axis=0, keepdims=True)
    low = low_ref[...].astype(F32)
    grad_middle = low + normalize_back(grad_second, normed, scale, vecs[FEED_GAIN : FEED_GAIN + 1])
    grad_middle_ref[...] = grad_middle
    grad_branch = grad_middle.astype(BF)
    grad_mixed_ref[...] = dot_nt(grad_branch, merge_ref[...]).astype(BF)
    merge_grad_ref[: width // 2] = dot_tn(mixed0[...], grad_branch).astype(BF)
    merge_grad_ref[width // 2 :] = dot_tn(mixed1[...], grad_branch).astype(BF)
    merge_bias = jnp.sum(grad_branch.astype(F32), axis=0, keepdims=True)
    down_bias = jnp.sum(low, axis=0, keepdims=True)
    sums_ref[...] = jnp.concatenate(
        [merge_bias, gain, shift, down_bias, jnp.zeros((4, width), F32)], axis=0
    )


def turn(middle, branch, back, low, keep_column, vecs, mixed, merge):
    count, width = middle.shape
    return pl.pallas_call(
        turn_kernel,
        in_specs=[VMEM] * 9,
        out_specs=[VMEM] * 5,
        out_shape=[
            far((count, width), F32),
            far((count, width), F32),
            far((width, width), BF),
            far((count, width), BF),
            jax.ShapeDtypeStruct((8, width), F32),
        ],
        compiler_params=params(40),
        name="turn",
    )(middle, branch, back, low, keep_column, vecs, *mixed, merge)


def shed_kernel(pieces, depth, table, first_ref, merge_grad_ref, dq, dk, dv, mine, theirs, sums_ref, grad, sem_out):
    width = merge_grad_ref.shape[1]
    some = dq.shape[1]
    sums = []
    for part, piece in enumerate((dq, dk, dv)):
        grad[:, part * some : (part + 1) * some] = dot_tn(first_ref[...], piece[...]).astype(BF)
        sums.append(jnp.sum(piece[...].astype(F32), axis=0, keepdims=True))
    grad[:, 3 * some : 3 * some + width] = merge_grad_ref[...]
    grad[:, 3 * some + width :] = jnp.zeros((width, grad.shape[1] - 3 * some - width), BF)
    moves = copies_out(table, grad, mine, theirs, sem_out, pieces, depth, 0, mine.shape[2])
    for move in moves:
        move.start()
    sums_ref[...] = jnp.concatenate(sums + [jnp.zeros((5, some), F32)], axis=0)
    for move in moves:
        move.wait()


def shed(plan, table, pair, first, merge_grad, parts):
    width = merge_grad.shape[0]
    some = parts[0].shape[1]
    half = (3 * some + width + LANES) // 2
    blocks = far((width // pair, pair, half), BF)
    pieces, depth = (1, 1) if width == pair else (plan.pieces, plan.depth)
    return pl.pallas_call(
        functools.partial(shed_kernel, pieces, depth),
        in_specs=[SMEM] + [VMEM] * 5,
        out_specs=[ANY] * 2 + [VMEM],
        out_shape=[blocks, blocks, jax.ShapeDtypeStruct((8, some), F32)],
        scratch_shapes=[pltpu.VMEM((width, 2 * half), BF), pltpu.SemaphoreType.DMA],
        compiler_params=params(32),
        name="shed",
    )(table, first, merge_grad, *parts)


def last_kernel(pieces, depth, table, rows_ref, first_ref, weight_ref, vec_ref, grad_middle_ref, sums_a, sums_b, *refs):
    sums_feed = refs[:QUARTERS]
    parts = refs[QUARTERS : QUARTERS + 6]
    high_ref, low_ref, mine, theirs, grad, sem_out = refs[QUARTERS + 6 :]
    count, width = rows_ref.shape
    some = parts[0].shape[1]
    vecs = vec_ref[...]
    sums = []
    for part in range(3):
        piece = parts[3 + part]
        grad[:, part * some : (part + 1) * some] = dot_tn(first_ref[...], piece[...]).astype(BF)
        sums.append(jnp.sum(piece[...].astype(F32), axis=0, keepdims=True))
    gain = jnp.zeros((1, width), F32)
    shift = jnp.zeros((1, width), F32)
    step = 256 if count % 256 == 0 else count
    for m in range(0, count, step):
        rows = slice(m, m + step)
        grad_first = jnp.zeros((step, width), F32)
        for side in range(2):
            for part in range(3):
                at = part * width + side * some
                grad_first = grad_first + dot_nt(parts[3 * side + part][rows], weight_ref[:, at : at + some])
        normed, scale = normalize(rows_ref[rows].astype(F32))
        gain = gain + jnp.sum(grad_first * normed, axis=0, keepdims=True)
        shift = shift + jnp.sum(grad_first, axis=0, keepdims=True)
        grad_rows = grad_middle_ref[rows] + normalize_back(
            grad_first, normed, scale, vecs[ATTEND_GAIN : ATTEND_GAIN + 1]
        )
        high = grad_rows.astype(BF)
        high_ref[rows] = high
        low_ref[rows] = (grad_rows - high.astype(F32)).astype(BF)
    query = jnp.concatenate([sums_a[0:1], sums[0]], axis=1)
    value = jnp.concatenate([sums_a[2:3], sums[2]], axis=1)
    lines = [gain, shift, query, value] + [sums_b[i : i + 1] for i in range(4)]
    lines += [x[0:1] for x in sums_feed]
    lines.append(jnp.zeros((LANES - len(lines), width), F32))
    grad[:, 3 * some :] = jnp.concatenate(lines, axis=0).T.astype(BF)
    moves = copies_out(table, grad, mine, theirs, sem_out, pieces, depth, 0, mine.shape[2])
    for move in moves:
        move.start()
    for move in moves:
        move.wait()


def last(plan, table, pair, rows, first, weight, vecs, grad_middle, sums, parts):
    count, width = rows.shape
    some = parts[0].shape[1]
    half = (3 * some + LANES) // 2
    blocks = far((width // pair, pair, half), BF)
    pieces, depth = (1, 1) if width == pair else (plan.pieces, plan.depth)
    return pl.pallas_call(
        functools.partial(last_kernel, pieces, depth),
        in_specs=[SMEM] + [VMEM] * (5 + len(sums) + len(parts)),
        out_specs=[VMEM] * 2 + [ANY] * 2,
        out_shape=[jax.ShapeDtypeStruct((count, width), BF)] * 2 + [blocks] * 2,
        scratch_shapes=[pltpu.VMEM((width, 2 * half), BF), pltpu.SemaphoreType.DMA],
        compiler_params=params(40),
        name="last",
    )(table, rows, first, weight, vecs, grad_middle, *sums, *parts)


def on_device(plan, cube_tokens, visible, padding, *rest):
    (
        attend_gain,
        attend_shift,
        triple_weight,
        query_bias,
        value_bias,
        merge_weight,
        merge_bias,
        feed_gain,
        feed_shift,
        up_weight,
        up_bias,
        down_weight,
        down_bias,
        cotangent,
    ) = rest
    slots, tokens, width = cube_tokens.shape
    length = visible.shape[1]
    count = slots * length
    devices = plan.depth * plan.inner
    share = width // devices
    table = plan.table()
    _, _, core = plan.position()
    direct = 2 * share % 16 == 0

    vectors = [attend_gain, attend_shift, query_bias, value_bias, merge_bias, feed_gain, feed_shift, down_bias]
    vectors = jnp.concatenate([jnp.stack(vectors), up_bias.reshape(QUARTERS, share)])

    def pieces_of(gather):
        own, other = gather.pieces()
        if direct:
            return own, other
        blocks = [jnp.concatenate(x).reshape(plan.chips, 2 * share, -1) for x in (own, other)]
        halves = []
        for side in (0, 1):
            order = jnp.argsort(table[side * plan.chips : (side + 1) * plan.chips])
            halves.append(blocks[side][order].reshape(1, width, -1))
        return [halves[0]], [halves[1]]

    def scatter_of(mine, theirs):
        if not direct:
            blocks = []
            for side, x in enumerate((mine, theirs)):
                order = table[side * plan.chips : (side + 1) * plan.chips]
                blocks.append(x.reshape(plan.chips, 2 * share, -1)[order])
            mine, theirs = blocks
        return Scatter(plan, mine, theirs)

    kernel_table = table if direct else jnp.stack([jnp.int32(0), jnp.int32(0), core.astype(jnp.int32)])
    pair = 2 * share if direct else width
    keep_row = padding.reshape(slots, 1, length)
    keep_column = padding.reshape(count, 1).astype(F32)
    cot = cotangent.reshape(count, width)
    stages = plan.bits

    cut = 3 * width // 2
    (block,) = chip_block(plan, pack(triple_weight, vectors), ())
    (one,) = Gather.column(plan, block, ())
    shard = part(tie(up_weight, block), down_weight, merge_weight)
    block_two, block_more = chip_block(plan, shard, (cut,))
    rows = pick_rows(cube_tokens, tie(visible, block_two))
    one.hold(rows)
    one.meet(0)
    (two,) = Gather.column(plan, block_two, (), one.own[0])
    one.share(0)
    for stage in range(1, stages):
        one.meet(stage)
        one.share(stage)
    one.share(stages)
    landed = tuple(one.other.values())
    three, four = Gather.column(plan, block_more, (width,), two.own[0])
    two.hold(*landed)
    two.meet(0)
    two.share(0)
    first, triple, weight, vecs = project(plan, kernel_table, tie(rows, two.own[0]), *pieces_of(one))
    mixed, probs = [None, None], [None, None]
    for stage in range(1, stages):
        two.meet(stage, triple)
        two.share(stage, triple)
    three.hold(triple)
    three.meet(0)
    three.share(0)
    four.hold(triple)
    mixed[0], probs[0] = attend(tie(triple, three.own[0]), keep_row, 0)
    two.share(stages, mixed[0])
    for stage in range(1, stages):
        three.meet(stage, mixed[0])
        three.share(stage, mixed[0])
    four.hold(mixed[0])
    four.meet(0)
    four.share(0)
    mixed[1], probs[1] = attend(tie(triple, *two.own.values(), *three.own.values()), keep_row, 1)
    pieces = pieces_of(two)
    middle, second, low, merge_weights = merge(
        kernel_table, width, rows, mixed, cot, keep_column, vecs, *pieces
    )
    three.share(stages, second)
    branch, back, mine, theirs, sums0 = feed(
        kernel_table, 0, 0, 0, second, low, vecs, (), (), *pieces, 2
    )
    for stage in range(1, stages):
        four.meet(stage, branch)
        four.share(stage, branch)
    pieces = pieces_of(three)
    branch, back, mine, theirs, sums1 = feed(
        kernel_table, 1, 0, 1, tie(second, *four.own.values()), low, vecs, (branch, back), (mine, theirs), *pieces, 2
    )
    four.share(stages, branch)
    pieces = pieces_of(four)
    early = scatter_of(mine, theirs)
    branch, back, mine, theirs, sums2 = feed(
        kernel_table, 2, 0, 0, second, low, vecs, (branch, back), (), *pieces, 2
    )
    early.meet(branch)
    branch, back, mine, theirs, sums3 = feed(
        kernel_table, 3, 1, 1, tie(second, early.sent), low, vecs, (branch, back), (mine, theirs), *pieces, 2
    )
    later = scatter_of(mine, theirs)
    output, grad_middle, merge_grad, grad_mixed, sums_turn = turn(
        middle, branch, back, low, keep_column, vecs, mixed, merge_weights
    )
    for _ in range(1, stages):
        early.meet(grad_mixed)
    later.meet(grad_mixed)
    parts = attend_back(triple, probs[0], mixed[0], tie(grad_mixed, early.sent, later.sent), 0)
    early.column(*parts)
    mine, theirs, sums_shed = shed(plan, kernel_table, pair, tie(first, early.sent), merge_grad, parts)
    front = scatter_of(mine, theirs)
    more = attend_back(triple, probs[1], mixed[1], tie(grad_mixed, mine), 1)
    for _ in range(1, stages):
        later.meet(*more)
    front.meet(*more)
    high, low_part, mine, theirs = last(
        plan,
        kernel_table,
        pair,
        tie(rows, later.sent, front.sent),
        first,
        weight,
        vecs,
        grad_middle,
        (sums_shed, sums_turn, sums0, sums1, sums2, sums3),
        list(parts) + list(more),
    )
    tail = scatter_of(mine, theirs)
    later.column(high)
    for _ in range(1, stages):
        front.meet(high)
    cube_gradient = spread_rows(visible, tie(high, later.sent, front.sent), low_part, tokens)
    front.column(cube_gradient)
    for _ in range(stages):
        tail.meet()
    tail.column()
    up_weight_grad, down_weight_grad = weave(early.finish(), later.finish())
    front, tail = front.finish(), tail.finish()

    some = width // 2
    triple_weight_grad = jnp.concatenate(
        [x[:, p * some : (p + 1) * some] for p in range(3) for x in (front, tail)], axis=1
    )
    merge_weight_grad = front[:, 3 * some : 3 * some + width]
    vector_grads = tail[:, 3 * some : 3 * some + VECS].T
    return (
        output.reshape(slots, length, width),
        cube_gradient,
        vector_grads[ATTEND_GAIN],
        vector_grads[ATTEND_SHIFT],
        triple_weight_grad,
        vector_grads[QUERY_BIAS],
        vector_grads[VALUE_BIAS],
        merge_weight_grad,
        vector_grads[MERGE_BIAS],
        vector_grads[FEED_GAIN],
        vector_grads[FEED_SHIFT],
        up_weight_grad,
        vector_grads[UP_BIAS : UP_BIAS + QUARTERS].reshape(QUARTERS * share),
        down_weight_grad,
        vector_grads[DOWN_BIAS],
    )


def solution(mesh):
    flat, matrix, cube = P(BOTH), P(BOTH, None), P(BOTH, None, None)
    return jax.shard_map(
        functools.partial(on_device, Plan(mesh)),
        mesh=mesh,
        in_specs=(
            cube,
            matrix,
            matrix,
            flat,
            flat,
            matrix,
            flat,
            flat,
            matrix,
            flat,
            flat,
            flat,
            matrix,
            flat,
            matrix,
            flat,
            cube,
        ),
        out_specs=(
            cube,
            cube,
            flat,
            flat,
            matrix,
            flat,
            flat,
            matrix,
            flat,
            flat,
            flat,
            matrix,
            flat,
            matrix,
            flat,
        ),
        check_vma=False,
    )
```

time: 847 us -> 302 us (0.36); the launches traced: 833 us -> 298 us
  waiting for transfers between devices: 388 us -> 94 us
  matrix products: 140 us -> 0 us
  other arithmetic: 139 us -> 10.6 us
  Pallas kernels: 0 us -> 116 us
  blocking collectives: 83.7 us -> 0 us
  starting transfers between devices: 0.32 us -> 60.9 us
  local copies, waits for them, and re-layouts: 66.7 us -> 15.1 us
  between operations: 15.4 us -> 1.96 us
    reduce_scatter x4 -> x0, waiting for transfers between devices: 287 us -> none  [the longest x1 142 us: reduce_gradients(): lax.psum_scatter(grads[11], ('gx', 'gy'), scatter_dimension=0, tiled=True)]
    dot_general x18 -> x0, matrix products: 140 us -> none  [the longest x1 27.1 us: forward_pass(): jnp.dot(second_low, up_weight, preferred_element_type=jnp.float32)]
    pallas_call x0 -> x18, Pallas kernels: none -> 116 us  [the longest x4 42.9 us: feed(): pl.pallas_call(functools.partial(feed_kernel, pieces, depth, quarter, at,...]
    scatter-add x1 -> x0, other arithmetic: 103 us -> none  [on_device(): jnp.zeros(cube_tokens.shape, jnp.float32).at[picked, visible].add(grad_rows)]
    all_gather x4 -> x0, waiting for transfers between devices: 98.3 us -> none  [the longest x1 57.1 us: fetch_weights(): lax.all_gather(up_weight, ('gx', 'gy'), axis=0, tiled=True)]
    ppermute x0 -> x67, waiting for transfers between devices: none -> 94 us  [the longest x21 42.2 us: shift(): return lax.ppermute(x, BOTH, pairs)]
    unnamed x2 -> x0, blocking collectives: 83.7 us -> none
    ppermute x0 -> x67, starting transfers between devices: none -> 60.9 us  [the longest x21 33.4 us: shift(): return lax.ppermute(x, BOTH, pairs)]
  transfers between devices with their start and end apart: 8 -> 67, of which waited for: 6 -> 26; matrix products, arithmetic and copies ran while one was open for 34% -> 4% of each run, Pallas kernels for 0% -> 30%
where the time goes in v1:
time: 302 us; the launch traced here: 298 us
  Pallas kernels  116 us (38%)
  waiting for transfers between devices  94 us (31%)
  starting transfers between devices  60.9 us (20%)
  local copies, waits for them, and re-layouts  15.1 us (5%)
  other arithmetic  10.6 us (4%)
    pallas_call x4, Pallas kernels, feed(): pl.pallas_call(functools.partial(feed_kernel, pieces, depth, quarter, at,...  42.9 us
    ppermute x21, waiting for transfers between devices, shift(): return lax.ppermute(x, BOTH, pairs)  42.2 us
    ppermute x20, waiting for transfers between devices, swap_place(): return lax.ppermute(x, BOTH, pairs)  40.6 us
    ppermute x21, starting transfers between devices, shift(): return lax.ppermute(x, BOTH, pairs)  33.4 us
    ppermute x20, starting transfers between devices, swap_place(): return lax.ppermute(x, BOTH, pairs)  22.9 us
    pallas_call x2, Pallas kernels, attend(): pl.pallas_call(attend_kernel, grid=(slots, some), in_specs=[pl.BlockSpec(...  15.7 us
    pallas_call x2, Pallas kernels, attend_back(): pl.pallas_call(attend_back_kernel, grid=(steps // some, some), in_specs=[...  12.1 us
    ppermute x26, waiting for transfers between devices, swap_core(): return lax.ppermute(x, BOTH, pairs)  11.1 us
  transfers between devices with their start and end apart: 67, of which 26 were waited for; matrix products, arithmetic and copies ran while one was open for 4% of the time, Pallas kernels for 30%

profile of v1, /device:TPU:0, one launch (start us, length us, event | category | flops | bytes accessed | tf_op | source)
XLA Modules:
  0.0 298.4 jit_solution(14046396280977483051)
XLA Ops:
  4.7 5.0 %collective-permute-start.4 = (bf16[48,1280]{1,0:T(8,128)(2,1)S(1)}, bf16[48,1280]{1,0:T(8,128)(2,1)S(1)}, u32[]{:S(2)}, u32[]{:S(2)}) collective-permute-start(bf16[48,1280]{1,0:T(8,128)(2,1)S(1)} %maximum_select_fusion.4), channel_id=1, source_target_pairs={{0,24},{1,25},{2,26},{3,27},{4,28},{5,29},{6,30},{7,31},{8,0},{9,1... | collective-permute-start | bytes 368648 | tf_op jit(solution)/shard_map/ppermute | solution.py:79
  13.7 7.0 %collective-permute-done.3 = bf16[48,1280]{1,0:T(8,128)(2,1)S(1)} collective-permute-done((bf16[48,1280]{1,0:T(8,128)(2,1)S(1)}, bf16[48,1280]{1,0:T(8,128)(2,1)S(1)}, u32[]{:S(2)}, u32[]{:S(2)}) %collective-permute-start.3) | collective-permute-done | bytes 122912 | tf_op jit(solution)/shard_map/ppermute | solution.py:79
  21.1 4.0 %pick.1.rows_ref = bf16[768,768]{1,0:T(8,128)(2,1)S(1)} custom-call(bf16[2,1536,768]{2,1,0:T(8,128)(2,1)} %cube_ref.1, s32[2,384,1]{2,1,0:T(8,128)S(1)} %copy.43.seen_ref), custom_call_target="tpu_custom_call" | custom-call | tf_op jit(solution)/shard_map/pick/pallas_call | solution.py:377
  25.1 1.5 collective-permute-start.7
  27.6 1.9 collective-permute-start.5
  29.8 1.6 collective-permute-start.9
  31.4 1.6 collective-permute-start.11
  33.0 4.2 %collective-permute-done.6 = bf16[48,1152]{1,0:T(8,128)(2,1)S(1)} collective-permute-done((bf16[48,1152]{1,0:T(8,128)(2,1)S(1)}, bf16[48,1152]{1,0:T(8,128)(2,1)S(1)}, u32[]{:S(2)}, u32[]{:S(2)}) %collective-permute-start.6) | collective-permute-done | bytes 110624 | tf_op jit(solution)/shard_map/ppermute | solution.py:79
  38.5 1.4 collective-permute-start.16
  39.9 4.5 %collective-permute-done.17 = bf16[48,2304]{1,0:T(8,128)(2,1)S(1)} collective-permute-done((bf16[48,2304]{1,0:T(8,128)(2,1)S(1)}, bf16[48,2304]{1,0:T(8,128)(2,1)S(1)}, u32[]{:S(2)}, u32[]{:S(2)}) %collective-permute-start.17) | collective-permute-done | bytes 221216 | tf_op jit(solution)/shard_map/ppermute | solution.py:79
  44.4 3.1 %collective-permute-start.15 = (bf16[48,2304]{1,0:T(8,128)(2,1)S(1)}, bf16[48,2304]{1,0:T(8,128)(2,1)S(1)}, u32[]{:S(2)}, u32[]{:S(2)}) collective-permute-start(bf16[48,2304]{1,0:T(8,128)(2,1)S(1)} %slice.485), channel_id=1, source_target_pairs={{0,8},{1,9},{2,10},{3,11},{4,12},{5,13},{6,14},{7,15},{8,16},{9,17... | collective-permute-start | bytes 663560 | tf_op jit(solution)/shard_map/ppermute | solution.py:79
  47.5 1.5 collective-permute-start.13
  49.0 10.5 %collective-permute-done.16 = bf16[48,2304]{1,0:T(8,128)(2,1)S(1)} collective-permute-done((bf16[48,2304]{1,0:T(8,128)(2,1)S(1)}, bf16[48,2304]{1,0:T(8,128)(2,1)S(1)}, u32[]{:S(2)}, u32[]{:S(2)}) %collective-permute-start.16) | collective-permute-done | bytes 221216 | tf_op jit(solution)/shard_map/ppermute | solution.py:79
  60.3 1.2 collective-permute-done.10.refs_5_
  62.9 1.5 collective-permute-start.18
  64.4 1.5 collective-permute-start.19
  66.0 7.6 %project.1 = (bf16[768,768]{1,0:T(8,128)(2,1)}, bf16[768,2304]{1,0:T(8,128)(2,1)}, bf16[768,2304]{1,0:T(8,128)(2,1)}, f32[16,768]{1,0:T(8,128)S(1)}) custom-call(s32[33]{0:T(128)S(1)} %stack.193.table, bf16[768,768]{1,0:T(8,128)(2,1)S(1)} %pick.1.rows_ref, bf16[4,48,1280]{2,1,0:T(8,128)(2,1)S(1)} %pad_maximum_fusion.1.refs_0_, ...), custom_call_target="tpu_custom_call" | custom-call | tf_op jit(solution)/shard_map/project/pallas_call | solution.py:448
  74.2 1.4 collective-permute-done.18.refs_1_
  75.6 1.4 collective-permute-start.20
  78.6 2.0 copy-done
  80.6 7.9 %attend.2 = (bf16[768,384]{1,0:T(8,128)(2,1)S(1)}, bf16[6,2,384,384]{3,2,1,0:T(8,128)(2,1)}) custom-call(bf16[768,2304]{1,0:T(8,128)(2,1)S(1)} %copy-done, bf16[768,2304]{1,0:T(8,128)(2,1)S(1)} %copy-done, bf16[768,2304]{1,0:T(8,128)(2,1)S(1)} %copy-done, s32[2,1,384]{2,1,0:T(1,128)S(1)} %reshape.146.keep_ref), custom_call_target="tpu_custom_call" | custom-call | tf_op jit(solution)/shard_map/attend/pallas_call | solution.py:491
  89.3 1.6 collective-permute-start.28
  90.8 1.4 collective-permute-start.23
  93.6 6.2 %collective-permute-done.23.refs_3_ = bf16[4,48,768]{2,1,0:T(8,128)(2,1)S(1)} collective-permute-done((bf16[4,48,768]{2,1,0:T(8,128)(2,1)S(1)}, bf16[4,48,768]{2,1,0:T(8,128)(2,1)S(1)}, u32[]{:S(2)}, u32[]{:S(2)}) %collective-permute-start.23) | collective-permute-done | bytes 294944 | tf_op jit(solution)/shard_map/ppermute | solution.py:74
  99.8 1.5 collective-permute-start.29
  102.4 7.9 %attend.3 = (bf16[768,384]{1,0:T(8,128)(2,1)S(1)}, bf16[6,2,384,384]{3,2,1,0:T(8,128)(2,1)}) custom-call(bf16[768,2304]{1,0:T(8,128)(2,1)S(1)} %copy-done.1, bf16[768,2304]{1,0:T(8,128)(2,1)S(1)} %copy-done.1, bf16[768,2304]{1,0:T(8,128)(2,1)S(1)} %copy-done.1, s32[2,1,384]{2,1,0:T(1,128)S(1)} %reshape.146.keep_ref), custom_call_target="tpu_custom_call" | custom-call | tf_op jit(solution)/shard_map/attend/pallas_call | solution.py:491
  110.3 4.7 %merge.1 = (f32[768,768]{1,0:T(8,128)}, bf16[768,768]{1,0:T(8,128)(2,1)S(1)}, bf16[768,768]{1,0:T(8,128)(2,1)S(1)}, bf16[768,768]{1,0:T(8,128)(2,1)}) custom-call(s32[33]{0:T(128)S(1)} %stack.193.table, bf16[768,768]{1,0:T(8,128)(2,1)S(1)} %copy-done.3, bf16[768,384]{1,0:T(8,128)(2,1)S(1)} %copy-done.5, ...), custom_call_target="tpu_custom_call" | custom-call | tf_op jit(solution)/shard_map/merge/pallas_call | solution.py:586
  115.1 10.5 %feed.4 = (f32[768,768]{1,0:T(8,128)S(1)}, f32[768,768]{1,0:T(8,128)S(1)}, bf16[16,48,1536]{2,1,0:T(8,128)(2,1)}, bf16[16,48,1536]{2,1,0:T(8,128)(2,1)}, f32[8,768]{1,0:T(8,128)S(1)}) custom-call(s32[33]{0:T(128)S(1)} %stack.193.table, bf16[768,768]{1,0:T(8,128)(2,1)S(1)} %get-tuple-element.149.second, bf16[768,768]{1,0:T(8,128)(2,1)S(1)} %get-tuple-element.132.low.low_ref, ...), custom_call_target="tpu_custom_call" | custom-call | tf_op jit(solution)/shard_map/feed/pallas_call | solution.py:653
  127.5 8.3 %collective-permute-done.30.refs_3_ = bf16[4,48,1536]{2,1,0:T(8,128)(2,1)S(1)} collective-permute-done((bf16[4,48,1536]{2,1,0:T(8,128)(2,1)}, bf16[4,48,1536]{2,1,0:T(8,128)(2,1)S(1)}, u32[]{:S(2)}, u32[]{:S(2)}) %collective-permute-start.30) | collective-permute-done | bytes 589856 | tf_op jit(solution)/shard_map/ppermute | solution.py:74
  135.8 10.5 %feed.5 = (f32[768,768]{1,0:T(8,128)S(1)}, f32[768,768]{1,0:T(8,128)S(1)}, bf16[16,48,1536]{2,1,0:T(8,128)(2,1)}, bf16[16,48,1536]{2,1,0:T(8,128)(2,1)}, f32[8,768]{1,0:T(8,128)S(1)}) custom-call(s32[33]{0:T(128)S(1)} %stack.193.table, ...), custom_call_target="tpu_custom_call", output_to_operand_aliasing={{0}: (12, {}), {1}: (13, {}), {2}: (14, {}), {3}: (15, {})} | custom-call | tf_op jit(solution)/shard_map/feed/pallas_call | solution.py:653
  147.5 5.3 %collective-permute-done.36.refs_4_ = bf16[4,48,1536]{2,1,0:T(8,128)(2,1)S(1)} collective-permute-done((bf16[4,48,1536]{2,1,0:T(8,128)(2,1)}, bf16[4,48,1536]{2,1,0:T(8,128)(2,1)S(1)}, u32[]{:S(2)}, u32[]{:S(2)}) %collective-permute-start.36) | collective-permute-done | bytes 589856 | tf_op jit(solution)/shard_map/ppermute | solution.py:67
  154.6 10.9 %feed.6 = (f32[768,768]{1,0:T(8,128)S(1)}, f32[768,768]{1,0:T(8,128)S(1)}, bf16[16,48,1536]{2,1,0:T(8,128)(2,1)}, bf16[16,48,1536]{2,1,0:T(8,128)(2,1)}, f32[8,768]{1,0:T(8,128)S(1)}) custom-call(s32[33]{0:T(128)S(1)} %stack.193.table, bf16[768,768]{1,0:T(8,128)(2,1)S(1)} %get-tuple-element.149.second, ...), custom_call_target="tpu_custom_call", output_to_operand_aliasing={{0}: (12, {}), {1}: (13, {})} | custom-call | tf_op jit(solution)/shard_map/feed/pallas_call | solution.py:653
  165.8 11.0 %feed.7 = (f32[768,768]{1,0:T(8,128)S(1)}, f32[768,768]{1,0:T(8,128)S(1)}, bf16[16,48,1536]{2,1,0:T(8,128)(2,1)}, bf16[16,48,1536]{2,1,0:T(8,128)(2,1)}, f32[8,768]{1,0:T(8,128)S(1)}) custom-call(s32[33]{0:T(128)S(1)} %stack.193.table, ...), custom_call_target="tpu_custom_call", output_to_operand_aliasing={{0}: (12, {}), {1}: (13, {}), {2}: (14, {}), {3}: (15, {})} | custom-call | tf_op jit(solution)/shard_map/feed/pallas_call | solution.py:653
  177.7 6.8 %turn.1 = (f32[768,768]{1,0:T(8,128)}, f32[768,768]{1,0:T(8,128)}, bf16[768,768]{1,0:T(8,128)(2,1)}, bf16[768,768]{1,0:T(8,128)(2,1)}, f32[8,768]{1,0:T(8,128)S(1)}) custom-call(f32[768,768]{1,0:T(8,128)S(1)} %copy-done.16, f32[768,768]{1,0:T(8,128)S(1)} %get-tuple-element.153.branch_ref, f32[768,768]{1,0:T(8,128)S(1)} %get-tuple-element.154.back_ref, ...), custom_call_target="tpu_custom_call" | custom-call | tf_op jit(solution)/shard_map/turn/pallas_call | solution.py:712
  184.5 8.8 %collective-permute-done.42 = bf16[8,48,1536]{2,1,0:T(8,128)(2,1)} collective-permute-done((bf16[8,48,1536]{2,1,0:T(8,128)(2,1)S(1)}, bf16[8,48,1536]{2,1,0:T(8,128)(2,1)}, u32[]{:S(2)}, u32[]{:S(2)}) %collective-permute-start.42) | collective-permute-done | bytes 1179680 | tf_op jit(solution)/shard_map/ppermute | solution.py:74
  193.3 1.3 add_convert_fusion.3
  195.6 1.5 copy-done.37
  198.2 11.8 %collective-permute-done.43 = bf16[4,48,1536]{2,1,0:T(8,128)(2,1)S(1)} collective-permute-done((bf16[4,48,1536]{2,1,0:T(8,128)(2,1)S(1)}, bf16[4,48,1536]{2,1,0:T(8,128)(2,1)S(1)}, u32[]{:S(2)}, u32[]{:S(2)}) %collective-permute-start.43) | collective-permute-done | bytes 589856 | tf_op jit(solution)/shard_map/ppermute | solution.py:74
  210.0 1.3 add_convert_fusion.11
  211.4 6.1 %attend_back.2 = (bf16[768,384]{1,0:T(8,128)(2,1)S(1)}, bf16[768,384]{1,0:T(8,128)(2,1)S(1)}, bf16[768,384]{1,0:T(8,128)(2,1)S(1)}) custom-call(bf16[768,2304]{1,0:T(8,128)(2,1)S(1)} %copy-done.1, bf16[768,2304]{1,0:T(8,128)(2,1)S(1)} %copy-done.1, bf16[768,2304]{1,0:T(8,128)(2,1)S(1)} %copy-done.1, bf16[6,2,384,384]{3,2,1,0:T(8,128)(2,1)S(1)} %copy-done.12, ...), custom_call_target="tpu_custom_call" | custom-call | tf_op jit(solution)/shard_map/attend_back/pallas_call | solution.py:541
  218.7 2.8 collective-permute-start.59
  221.5 4.3 %shed.1 = (bf16[16,48,1024]{2,1,0:T(8,128)(2,1)}, bf16[16,48,1024]{2,1,0:T(8,128)(2,1)}, f32[8,384]{1,0:T(8,128)S(1)}) custom-call(s32[33]{0:T(128)S(1)} %stack.193.table, bf16[768,768]{1,0:T(8,128)(2,1)S(1)} %copy-done.6, bf16[768,768]{1,0:T(8,128)(2,1)S(1)} %copy-done.23, bf16[768,384]{1,0:T(8,128)(2,1)S(1)} %get-tuple-element.166.dq.refs_4_, ...), custom_call_target="tpu_custom_call" | custom-call | tf_op jit(solution)/shard_map/shed/pallas_call | solution.py:751
  225.9 6.0 %attend_back.3 = (bf16[768,384]{1,0:T(8,128)(2,1)S(1)}, bf16[768,384]{1,0:T(8,128)(2,1)S(1)}, bf16[768,384]{1,0:T(8,128)(2,1)S(1)}) custom-call(bf16[768,2304]{1,0:T(8,128)(2,1)S(1)} %copy-done.1, bf16[768,2304]{1,0:T(8,128)(2,1)S(1)} %copy-done.1, bf16[768,2304]{1,0:T(8,128)(2,1)S(1)} %copy-done.1, bf16[6,2,384,384]{3,2,1,0:T(8,128)(2,1)S(1)} %copy-done.13, ...), custom_call_target="tpu_custom_call" | custom-call | tf_op jit(solution)/shard_map/attend_back/pallas_call | solution.py:541
  232.0 1.2 convert_add_fusion.1
  236.0 9.2 %last.1 = (bf16[768,768]{1,0:T(8,128)(2,1)S(1)}, bf16[768,768]{1,0:T(8,128)(2,1)S(1)}, bf16[16,48,640]{2,1,0:T(8,128)(2,1)}, bf16[16,48,640]{2,1,0:T(8,128)(2,1)}) custom-call(s32[33]{0:T(128)S(1)} %stack.193.table, bf16[768,768]{1,0:T(8,128)(2,1)S(1)} %copy-done.3, bf16[768,768]{1,0:T(8,128)(2,1)S(1)} %copy-done.6, bf16[768,2304]{1,0:T(8,128)(2,1)S(1)} %copy-done.11, ...), custom_call_target="tpu_custom_call" | custom-call | tf_op jit(solution)/shard_map/last/pallas_call | solution.py:812
  245.3 1.4 add_convert_fusion.8
  247.3 1.5 collective-permute-start.64
  248.8 3.1 %collective-permute-start.63 = (bf16[1,48,1536]{2,1,0:T(8,128)(2,1)S(1)}, bf16[1,48,1536]{2,1,0:T(8,128)(2,1)S(1)}, u32[]{:S(2)}, u32[]{:S(2)}) collective-permute-start(bf16[1,48,1536]{2,1,0:T(8,128)(2,1)S(1)} %get-tuple-element.201), channel_id=1, source_target_pairs={{0,24},{1,25},{2,26},{3,27},{4,28},{5,29},{6,30},{7,31},{8,0},{9,1... | collective-permute-start | bytes 442376 | tf_op jit(solution)/shard_map/ppermute | solution.py:79
  252.9 2.4 collective-permute-done.65
  255.4 5.8 %collective-permute-done.64 = bf16[1,48,1536]{2,1,0:T(8,128)(2,1)S(1)} collective-permute-done((bf16[1,48,1536]{2,1,0:T(8,128)(2,1)S(1)}, bf16[1,48,1536]{2,1,0:T(8,128)(2,1)S(1)}, u32[]{:S(2)}, u32[]{:S(2)}) %collective-permute-start.64) | collective-permute-done | bytes 147488 | tf_op jit(solution)/shard_map/ppermute | solution.py:79
  262.4 1.6 collective-permute-done.46
  266.3 1.3 weave.1
  267.6 7.0 %spread.1 = f32[2,1536,768]{2,1,0:T(8,128)} custom-call(s32[2,1,384]{2,1,0:T(1,128)S(1)} %reshape.149.seen_ref, bf16[768,768]{1,0:T(8,128)(2,1)S(1)} %get-tuple-element.192.high_ref, bf16[768,768]{1,0:T(8,128)(2,1)S(1)} %get-tuple-element.193.low_ref), custom_call_target="tpu_custom_call" | custom-call | tf_op jit(solution)/shard_map/spread/pallas_call | solution.py:403
  274.6 1.2 collective-permute-done.54
  275.9 1.9 collective-permute-start.57
  277.9 1.7 collective-permute-start.56
  281.3 1.3 collective-permute-done.57
  282.6 2.7 collective-permute-done.56
  285.5 1.2 collective-permute-done.49
  286.8 1.3 collective-permute-start.52
  288.1 1.2 collective-permute-start.51
  289.3 2.0 collective-permute-start.50
  291.3 2.1 collective-permute-done.52
  293.4 1.6 collective-permute-done.51
  (252 shorter events, 40.7 us)
Async XLA Ops:
  4.7 9.1 %collective-permute-start.4 = (bf16[48,1280]{1,0:T(8,128)(2,1)S(1)}, bf16[48,1280]{1,0:T(8,128)(2,1)S(1)}, u32[]{:S(2)}, u32[]{:S(2)}) collective-permute-start(bf16[48,1280]{1,0:T(8,128)(2,1)S(1)} %maximum_select_fusion.4), channel_id=1, source_target_pairs={{0,24},{1,25},{2,26},{3,27},{4,28},{5,29},{6,30},{7,31},{8,0},{9,1... | collective-permute-start | bytes 368648 | tf_op jit(solution)/shard_map/ppermute | solution.py:79
  9.7 11.1 %collective-permute-start.3 = (bf16[48,1280]{1,0:T(8,128)(2,1)S(1)}, bf16[48,1280]{1,0:T(8,128)(2,1)S(1)}, u32[]{:S(2)}, u32[]{:S(2)}) collective-permute-start(bf16[48,1280]{1,0:T(8,128)(2,1)S(1)} %maximum_select_fusion.4), channel_id=1, source_target_pairs={{0,16},{1,17},{2,18},{3,19},{4,20},{5,21},{6,22},{7,23},{8,24},{9,... | collective-permute-start | bytes 368648 | tf_op jit(solution)/shard_map/ppermute | solution.py:79
  9.7 11.1 %collective-permute-start.2 = (bf16[48,1280]{1,0:T(8,128)(2,1)S(1)}, bf16[48,1280]{1,0:T(8,128)(2,1)S(1)}, u32[]{:S(2)}, u32[]{:S(2)}) collective-permute-start(bf16[48,1280]{1,0:T(8,128)(2,1)S(1)} %maximum_select_fusion.4), channel_id=1, source_target_pairs={{0,8},{1,9},{2,10},{3,11},{4,12},{5,13},{6,14},{7,15},{8,16},{9,17... | collective-permute-start | bytes 368648 | tf_op jit(solution)/shard_map/ppermute | solution.py:79
  13.6 7.2 %collective-permute-start.1 = (bf16[24,3456]{1,0:T(8,128)(2,1)S(1)}, bf16[24,3456]{1,0:T(8,128)(2,1)S(1)}, u32[]{:S(2)}, u32[]{:S(2)}) collective-permute-start(bf16[24,3456]{1,0:T(8,128)(2,1)S(1)} %get-tuple-element.226), channel_id=1, source_target_pairs={{0,1},{1,0},{2,3},{3,2},{4,5},{5,4},{6,7},{7,6},{8,9},{9,8},{10,11... | collective-permute-start | bytes 497672 | tf_op jit(solution)/shard_map/ppermute | solution.py:67
  25.1 6.2 %collective-permute-start.7 = (bf16[48,1152]{1,0:T(8,128)(2,1)S(1)}, bf16[48,1152]{1,0:T(8,128)(2,1)S(1)}, u32[]{:S(2)}, u32[]{:S(2)}) collective-permute-start(bf16[48,1152]{1,0:T(8,128)(2,1)S(1)} %slice.484), channel_id=1, source_target_pairs={{0,24},{1,25},{2,26},{3,27},{4,28},{5,29},{6,30},{7,31},{8,0},{9,1... | collective-permute-start | bytes 331784 | tf_op jit(solution)/shard_map/ppermute | solution.py:79
  26.7 10.5 %collective-permute-start.6 = (bf16[48,1152]{1,0:T(8,128)(2,1)S(1)}, bf16[48,1152]{1,0:T(8,128)(2,1)S(1)}, u32[]{:S(2)}, u32[]{:S(2)}) collective-permute-start(bf16[48,1152]{1,0:T(8,128)(2,1)S(1)} %slice.484), channel_id=1, source_target_pairs={{0,16},{1,17},{2,18},{3,19},{4,20},{5,21},{6,22},{7,23},{8,24},{9,... | collective-permute-start | bytes 331784 | tf_op jit(solution)/shard_map/ppermute | solution.py:79
  27.6 9.5 %collective-permute-start.5 = (bf16[48,1152]{1,0:T(8,128)(2,1)S(1)}, bf16[48,1152]{1,0:T(8,128)(2,1)}, u32[]{:S(2)}, u32[]{:S(2)}) collective-permute-start(bf16[48,1152]{1,0:T(8,128)(2,1)S(1)} %slice.484), channel_id=1, source_target_pairs={{0,8},{1,9},{2,10},{3,11},{4,12},{5,13},{6,14},{7,15},{8,16},{9,17... | collective-permute-start | bytes 331784 | tf_op jit(solution)/shard_map/ppermute | solution.py:79
  29.7 30.6 %collective-permute-start.8 = (bf16[4,48,1280]{2,1,0:T(8,128)(2,1)S(1)}, bf16[4,48,1280]{2,1,0:T(8,128)(2,1)S(1)}, u32[]{:S(2)}, u32[]{:S(2)}) collective-permute-start(bf16[4,48,1280]{2,1,0:T(8,128)(2,1)S(1)} %pad_maximum_fusion.1.refs_0_), channel_id=1, source_target_pairs={{0,1},{1,0},{2,3},{3,2},{4,5},{5,4},{6,7},{7,6},{8,9},{9,8},{10,11... | collective-permute-start | bytes 1474568 | tf_op jit(solution)/shard_map/ppermute | solution.py:67
  29.8 17.7 %collective-permute-start.9 = (bf16[4,48,1280]{2,1,0:T(8,128)(2,1)S(1)}, bf16[4,48,1280]{2,1,0:T(8,128)(2,1)S(1)}, u32[]{:S(2)}, u32[]{:S(2)}) collective-permute-start(bf16[4,48,1280]{2,1,0:T(8,128)(2,1)S(1)} %pad_maximum_fusion.1.refs_0_), channel_id=1, source_target_pairs={{0,4},{1,3},{2,6},{3,1},{4,0},{5,7},{6,2},{7,5},{8,12},{9,11},{10,... | collective-permute-start | bytes 1474568 | tf_op jit(solution)/shard_map/ppermute | solution.py:74
  31.4 28.2 %collective-permute-start.11 = (bf16[4,48,1280]{2,1,0:T(8,128)(2,1)S(1)}, bf16[4,48,1280]{2,1,0:T(8,128)(2,1)S(1)}, u32[]{:S(2)}, u32[]{:S(2)}) collective-permute-start(bf16[4,48,1280]{2,1,0:T(8,128)(2,1)S(1)} %pad_maximum_fusion.1.refs_0_), channel_id=1, source_target_pairs={{0,2},{1,5},{2,0},{3,7},{4,6},{5,1},{6,4},{7,3},{8,10},{9,13},{10,... | collective-permute-start | bytes 1474568 | tf_op jit(solution)/shard_map/ppermute | solution.py:74
  38.1 6.3 %collective-permute-start.17 = (bf16[48,2304]{1,0:T(8,128)(2,1)S(1)}, bf16[48,2304]{1,0:T(8,128)(2,1)S(1)}, u32[]{:S(2)}, u32[]{:S(2)}) collective-permute-start(bf16[48,2304]{1,0:T(8,128)(2,1)S(1)} %slice.485), channel_id=1, source_target_pairs={{0,24},{1,25},{2,26},{3,27},{4,28},{5,29},{6,30},{7,31},{8,0},{9,1... | collective-permute-start | bytes 663560 | tf_op jit(solution)/shard_map/ppermute | solution.py:79
  38.5 21.0 %collective-permute-start.16 = (bf16[48,2304]{1,0:T(8,128)(2,1)S(1)}, bf16[48,2304]{1,0:T(8,128)(2,1)S(1)}, u32[]{:S(2)}, u32[]{:S(2)}) collective-permute-start(bf16[48,2304]{1,0:T(8,128)(2,1)S(1)} %slice.485), channel_id=1, source_target_pairs={{0,16},{1,17},{2,18},{3,19},{4,20},{5,21},{6,22},{7,23},{8,24},{9,... | collective-permute-start | bytes 663560 | tf_op jit(solution)/shard_map/ppermute | solution.py:79
  44.4 15.1 %collective-permute-start.15 = (bf16[48,2304]{1,0:T(8,128)(2,1)S(1)}, bf16[48,2304]{1,0:T(8,128)(2,1)S(1)}, u32[]{:S(2)}, u32[]{:S(2)}) collective-permute-start(bf16[48,2304]{1,0:T(8,128)(2,1)S(1)} %slice.485), channel_id=1, source_target_pairs={{0,8},{1,9},{2,10},{3,11},{4,12},{5,13},{6,14},{7,15},{8,16},{9,17... | collective-permute-start | bytes 663560 | tf_op jit(solution)/shard_map/ppermute | solution.py:79
  47.5 12.6 %collective-permute-start.13 = (bf16[4,48,1280]{2,1,0:T(8,128)(2,1)S(1)}, bf16[4,48,1280]{2,1,0:T(8,128)(2,1)S(1)}, u32[]{:S(2)}, u32[]{:S(2)}) collective-permute-start(bf16[4,48,1280]{2,1,0:T(8,128)(2,1)S(1)} %collective-permute-done.9.refs_1_), channel_id=1, source_target_pairs={{0,2},{1,5},{2,0},{3,7},{4,6},{5,1},{6,4},{7,3},{8,10},{9,13},{10,... | collective-permute-start | bytes 1474568 | tf_op jit(solution)/shard_map/ppermute | solution.py:74
  59.6 2.5 collective-permute-start.12
  60.1 2.8 collective-permute-start.14
  62.9 12.7 %collective-permute-start.18 = (bf16[4,48,1152]{2,1,0:T(8,128)(2,1)S(1)}, bf16[4,48,1152]{2,1,0:T(8,128)(2,1)}, u32[]{:S(2)}, u32[]{:S(2)}) collective-permute-start(bf16[4,48,1152]{2,1,0:T(8,128)(2,1)S(1)} %pad_maximum_fusion.2.refs_0_), channel_id=1, source_target_pairs={{0,4},{1,3},{2,6},{3,1},{4,0},{5,7},{6,2},{7,5},{8,12},{9,11},{10,... | collective-permute-start | bytes 1327112 | tf_op jit(solution)/shard_map/ppermute | solution.py:74
  64.4 26.4 %collective-permute-start.19 = (bf16[4,48,1152]{2,1,0:T(8,128)(2,1)S(1)}, bf16[4,48,1152]{2,1,0:T(8,128)(2,1)}, u32[]{:S(2)}, u32[]{:S(2)}) collective-permute-start(bf16[4,48,1152]{2,1,0:T(8,128)(2,1)S(1)} %pad_maximum_fusion.2.refs_0_), channel_id=1, source_target_pairs={{0,2},{1,5},{2,0},{3,7},{4,6},{5,1},{6,4},{7,3},{8,10},{9,13},{10,... | collective-permute-start | bytes 1327112 | tf_op jit(solution)/shard_map/ppermute | solution.py:74
  66.0 26.8 %collective-permute-start.24 = (bf16[4,48,1152]{2,1,0:T(8,128)(2,1)S(1)}, bf16[4,48,1152]{2,1,0:T(8,128)(2,1)S(1)}, u32[]{:S(2)}, u32[]{:S(2)}) collective-permute-start(bf16[4,48,1152]{2,1,0:T(8,128)(2,1)S(1)} %pad_maximum_fusion.2.refs_0_), channel_id=1, source_target_pairs={{0,1},{1,0},{2,3},{3,2},{4,5},{5,4},{6,7},{7,6},{8,9},{9,8},{10,11... | collective-permute-start | bytes 1327112 | tf_op jit(solution)/shard_map/ppermute | solution.py:67
  73.6 15.7 %collective-permute-start.21 = (bf16[4,48,768]{2,1,0:T(8,128)(2,1)S(1)}, bf16[4,48,768]{2,1,0:T(8,128)(2,1)S(1)}, u32[]{:S(2)}, u32[]{:S(2)}) collective-permute-start(bf16[4,48,768]{2,1,0:T(8,128)(2,1)S(1)} %pad_maximum_fusion.3.refs_0_), channel_id=1, source_target_pairs={{0,4},{1,3},{2,6},{3,1},{4,0},{5,7},{6,2},{7,5},{8,12},{9,11},{10,... | collective-permute-start | bytes 884744 | tf_op jit(solution)/shard_map/ppermute | solution.py:74
  75.6 16.6 %collective-permute-start.20 = (bf16[4,48,1152]{2,1,0:T(8,128)(2,1)}, bf16[4,48,1152]{2,1,0:T(8,128)(2,1)}, u32[]{:S(2)}, u32[]{:S(2)}) collective-permute-start(bf16[4,48,1152]{2,1,0:T(8,128)(2,1)} %collective-permute-done.18.refs_1_), channel_id=1, source_target_pairs={{0,2},{1,5},{2,0},{3,7},{4,6},{5,1},{6,4},{7,3},{8,10},{9,13},{10,... | collective-permute-start | bytes 1327112 | tf_op jit(solution)/shard_map/ppermute | solution.py:74
  77.0 15.2 %collective-permute-start.22 = (bf16[4,48,768]{2,1,0:T(8,128)(2,1)S(1)}, bf16[4,48,768]{2,1,0:T(8,128)(2,1)S(1)}, u32[]{:S(2)}, u32[]{:S(2)}) collective-permute-start(bf16[4,48,768]{2,1,0:T(8,128)(2,1)S(1)} %pad_maximum_fusion.3.refs_0_), channel_id=1, source_target_pairs={{0,2},{1,5},{2,0},{3,7},{4,6},{5,1},{6,4},{7,3},{8,10},{9,13},{10,... | collective-permute-start | bytes 884744 | tf_op jit(solution)/shard_map/ppermute | solution.py:74
  89.3 36.4 %collective-permute-start.28 = (bf16[4,48,1536]{2,1,0:T(8,128)(2,1)}, bf16[4,48,1536]{2,1,0:T(8,128)(2,1)}, u32[]{:S(2)}, u32[]{:S(2)}) collective-permute-start(bf16[4,48,1536]{2,1,0:T(8,128)(2,1)} %pad_maximum_fusion.refs_0_), channel_id=1, source_target_pairs={{0,4},{1,3},{2,6},{3,1},{4,0},{5,7},{6,2},{7,5},{8,12},{9,11},{10,... | collective-permute-start | bytes 1769480 | tf_op jit(solution)/shard_map/ppermute | solution.py:74
  90.8 9.0 %collective-permute-start.23 = (bf16[4,48,768]{2,1,0:T(8,128)(2,1)S(1)}, bf16[4,48,768]{2,1,0:T(8,128)(2,1)S(1)}, u32[]{:S(2)}, u32[]{:S(2)}) collective-permute-start(bf16[4,48,768]{2,1,0:T(8,128)(2,1)S(1)} %collective-permute-done.21.refs_1_), channel_id=1, source_target_pairs={{0,2},{1,5},{2,0},{3,7},{4,6},{5,1},{6,4},{7,3},{8,10},{9,13},{10,... | collective-permute-start | bytes 884744 | tf_op jit(solution)/shard_map/ppermute | solution.py:74
  92.2 18.0 %collective-permute-start.25 = (bf16[4,48,1152]{2,1,0:T(8,128)(2,1)}, bf16[4,48,1152]{2,1,0:T(8,128)(2,1)}, u32[]{:S(2)}, u32[]{:S(2)}) collective-permute-start(bf16[4,48,1152]{2,1,0:T(8,128)(2,1)} %collective-permute-done.18.refs_1_), channel_id=1, source_target_pairs={{0,1},{1,0},{2,3},{3,2},{4,5},{5,4},{6,7},{7,6},{8,9},{9,8},{10,11... | collective-permute-start | bytes 1327112 | tf_op jit(solution)/shard_map/ppermute | solution.py:67
  92.2 18.0 %collective-permute-start.26 = (bf16[4,48,1152]{2,1,0:T(8,128)(2,1)}, bf16[4,48,1152]{2,1,0:T(8,128)(2,1)}, u32[]{:S(2)}, u32[]{:S(2)}) collective-permute-start(bf16[4,48,1152]{2,1,0:T(8,128)(2,1)} %collective-permute-done.19.refs_2_), channel_id=1, source_target_pairs={{0,1},{1,0},{2,3},{3,2},{4,5},{5,4},{6,7},{7,6},{8,9},{9,8},{10,11... | collective-permute-start | bytes 1327112 | tf_op jit(solution)/shard_map/ppermute | solution.py:67
  93.5 16.7 %collective-permute-start.27 = (bf16[4,48,1152]{2,1,0:T(8,128)(2,1)}, bf16[4,48,1152]{2,1,0:T(8,128)(2,1)}, u32[]{:S(2)}, u32[]{:S(2)}) collective-permute-start(bf16[4,48,1152]{2,1,0:T(8,128)(2,1)} %collective-permute-done.20.refs_3_), channel_id=1, source_target_pairs={{0,1},{1,0},{2,3},{3,2},{4,5},{5,4},{6,7},{7,6},{8,9},{9,8},{10,11... | collective-permute-start | bytes 1327112 | tf_op jit(solution)/shard_map/ppermute | solution.py:67
  99.8 27.2 %collective-permute-start.29 = (bf16[4,48,1536]{2,1,0:T(8,128)(2,1)}, bf16[4,48,1536]{2,1,0:T(8,128)(2,1)}, u32[]{:S(2)}, u32[]{:S(2)}) collective-permute-start(bf16[4,48,1536]{2,1,0:T(8,128)(2,1)} %pad_maximum_fusion.refs_0_), channel_id=1, source_target_pairs={{0,2},{1,5},{2,0},{3,7},{4,6},{5,1},{6,4},{7,3},{8,10},{9,13},{10,... | collective-permute-start | bytes 1769480 | tf_op jit(solution)/shard_map/ppermute | solution.py:74
  125.6 10.2 %collective-permute-start.30 = (bf16[4,48,1536]{2,1,0:T(8,128)(2,1)}, bf16[4,48,1536]{2,1,0:T(8,128)(2,1)S(1)}, u32[]{:S(2)}, u32[]{:S(2)}) collective-permute-start(bf16[4,48,1536]{2,1,0:T(8,128)(2,1)} %collective-permute-done.28.refs_1_), channel_id=1, source_target_pairs={{0,2},{1,5},{2,0},{3,7},{4,6},{5,1},{6,4},{7,3},{8,10},{9,13},{10,... | collective-permute-start | bytes 1769480 | tf_op jit(solution)/shard_map/ppermute | solution.py:74
  126.4 9.4 %collective-permute-start.31 = (bf16[4,48,768]{2,1,0:T(8,128)(2,1)S(1)}, bf16[4,48,768]{2,1,0:T(8,128)(2,1)S(1)}, u32[]{:S(2)}, u32[]{:S(2)}) collective-permute-start(bf16[4,48,768]{2,1,0:T(8,128)(2,1)S(1)} %copy-done.21), channel_id=1, source_target_pairs={{0,1},{1,0},{2,3},{3,2},{4,5},{5,4},{6,7},{7,6},{8,9},{9,8},{10,11... | collective-permute-start | bytes 884744 | tf_op jit(solution)/shard_map/ppermute | solution.py:67
  126.4 9.4 %collective-permute-start.32 = (bf16[4,48,768]{2,1,0:T(8,128)(2,1)S(1)}, bf16[4,48,768]{2,1,0:T(8,128)(2,1)S(1)}, u32[]{:S(2)}, u32[]{:S(2)}) collective-permute-start(bf16[4,48,768]{2,1,0:T(8,128)(2,1)S(1)} %copy-done.26), channel_id=1, source_target_pairs={{0,1},{1,0},{2,3},{3,2},{4,5},{5,4},{6,7},{7,6},{8,9},{9,8},{10,11... | collective-permute-start | bytes 884744 | tf_op jit(solution)/shard_map/ppermute | solution.py:67
  126.9 8.9 %collective-permute-start.33 = (bf16[4,48,768]{2,1,0:T(8,128)(2,1)S(1)}, bf16[4,48,768]{2,1,0:T(8,128)(2,1)S(1)}, u32[]{:S(2)}, u32[]{:S(2)}) collective-permute-start(bf16[4,48,768]{2,1,0:T(8,128)(2,1)S(1)} %copy-done.28), channel_id=1, source_target_pairs={{0,1},{1,0},{2,3},{3,2},{4,5},{5,4},{6,7},{7,6},{8,9},{9,8},{10,11... | collective-permute-start | bytes 884744 | tf_op jit(solution)/shard_map/ppermute | solution.py:67
  127.0 8.8 %collective-permute-start.34 = (bf16[4,48,768]{2,1,0:T(8,128)(2,1)S(1)}, bf16[4,48,768]{2,1,0:T(8,128)(2,1)S(1)}, u32[]{:S(2)}, u32[]{:S(2)}) collective-permute-start(bf16[4,48,768]{2,1,0:T(8,128)(2,1)S(1)} %copy-done.30), channel_id=1, source_target_pairs={{0,1},{1,0},{2,3},{3,2},{4,5},{5,4},{6,7},{7,6},{8,9},{9,8},{10,11... | collective-permute-start | bytes 884744 | tf_op jit(solution)/shard_map/ppermute | solution.py:67
  146.4 19.1 %collective-permute-start.35 = (bf16[16,48,1536]{2,1,0:T(8,128)(2,1)}, bf16[16,48,1536]{2,1,0:T(8,128)(2,1)S(1)}, u32[]{:S(2)}, u32[]{:S(2)}) collective-permute-start(bf16[16,48,1536]{2,1,0:T(8,128)(2,1)} %get-tuple-element.142), channel_id=1, source_target_pairs={{0,1},{1,0},{2,3},{3,2},{4,5},{5,4},{6,7},{7,6},{8,9},{9,8},{10,11... | collective-permute-start | bytes 7077896 | tf_op jit(solution)/shard_map/ppermute | solution.py:67
  146.4 6.4 %collective-permute-start.36 = (bf16[4,48,1536]{2,1,0:T(8,128)(2,1)}, bf16[4,48,1536]{2,1,0:T(8,128)(2,1)S(1)}, u32[]{:S(2)}, u32[]{:S(2)}) collective-permute-start(bf16[4,48,1536]{2,1,0:T(8,128)(2,1)} %pad_maximum_fusion.refs_0_), channel_id=1, source_target_pairs={{0,1},{1,0},{2,3},{3,2},{4,5},{5,4},{6,7},{7,6},{8,9},{9,8},{10,11... | collective-permute-start | bytes 1769480 | tf_op jit(solution)/shard_map/ppermute | solution.py:67
  146.9 6.8 %collective-permute-start.37 = (bf16[4,48,1536]{2,1,0:T(8,128)(2,1)}, bf16[4,48,1536]{2,1,0:T(8,128)(2,1)S(1)}, u32[]{:S(2)}, u32[]{:S(2)}) collective-permute-start(bf16[4,48,1536]{2,1,0:T(8,128)(2,1)} %collective-permute-done.28.refs_1_), channel_id=1, source_target_pairs={{0,1},{1,0},{2,3},{3,2},{4,5},{5,4},{6,7},{7,6},{8,9},{9,8},{10,11... | collective-permute-start | bytes 1769480 | tf_op jit(solution)/shard_map/ppermute | solution.py:67
  147.0 7.5 %collective-permute-start.38 = (bf16[4,48,1536]{2,1,0:T(8,128)(2,1)}, bf16[4,48,1536]{2,1,0:T(8,128)(2,1)S(1)}, u32[]{:S(2)}, u32[]{:S(2)}) collective-permute-start(bf16[4,48,1536]{2,1,0:T(8,128)(2,1)} %collective-permute-done.29.refs_2_), channel_id=1, source_target_pairs={{0,1},{1,0},{2,3},{3,2},{4,5},{5,4},{6,7},{7,6},{8,9},{9,8},{10,11... | collective-permute-start | bytes 1769480 | tf_op jit(solution)/shard_map/ppermute | solution.py:67
  147.5 7.1 %collective-permute-start.39 = (bf16[4,48,1536]{2,1,0:T(8,128)(2,1)S(1)}, bf16[4,48,1536]{2,1,0:T(8,128)(2,1)S(1)}, u32[]{:S(2)}, u32[]{:S(2)}) collective-permute-start(bf16[4,48,1536]{2,1,0:T(8,128)(2,1)S(1)} %collective-permute-done.30.refs_3_), channel_id=1, source_target_pairs={{0,1},{1,0},{2,3},{3,2},{4,5},{5,4},{6,7},{7,6},{8,9},{9,8},{10,11... | collective-permute-start | bytes 1769480 | tf_op jit(solution)/shard_map/ppermute | solution.py:67
  176.8 18.8 %collective-permute-start.40 = (bf16[16,48,1536]{2,1,0:T(8,128)(2,1)}, bf16[16,48,1536]{2,1,0:T(8,128)(2,1)S(1)}, u32[]{:S(2)}, u32[]{:S(2)}) collective-permute-start(bf16[16,48,1536]{2,1,0:T(8,128)(2,1)} %get-tuple-element.158), channel_id=1, source_target_pairs={{0,1},{1,0},{2,3},{3,2},{4,5},{5,4},{6,7},{7,6},{8,9},{9,8},{10,11... | collective-permute-start | bytes 7077896 | tf_op jit(solution)/shard_map/ppermute | solution.py:67
  177.0 16.3 %collective-permute-start.42 = (bf16[8,48,1536]{2,1,0:T(8,128)(2,1)S(1)}, bf16[8,48,1536]{2,1,0:T(8,128)(2,1)}, u32[]{:S(2)}, u32[]{:S(2)}) collective-permute-start(bf16[8,48,1536]{2,1,0:T(8,128)(2,1)S(1)} %add_convert_fusion.1), channel_id=1, source_target_pairs={{0,2},{1,5},{2,0},{3,7},{4,6},{5,1},{6,4},{7,3},{8,10},{9,13},{10,... | collective-permute-start | bytes 3538952 | tf_op jit(solution)/shard_map/ppermute | solution.py:74
  194.6 15.4 %collective-permute-start.43 = (bf16[4,48,1536]{2,1,0:T(8,128)(2,1)S(1)}, bf16[4,48,1536]{2,1,0:T(8,128)(2,1)S(1)}, u32[]{:S(2)}, u32[]{:S(2)}) collective-permute-start(bf16[4,48,1536]{2,1,0:T(8,128)(2,1)S(1)} %add_convert_fusion.3), channel_id=1, source_target_pairs={{0,4},{1,3},{2,6},{3,1},{4,0},{5,7},{6,2},{7,5},{8,12},{9,11},{10,... | collective-permute-start | bytes 1769480 | tf_op jit(solution)/shard_map/ppermute | solution.py:74
  197.4 35.7 %collective-permute-start.41 = (bf16[8,48,1536]{2,1,0:T(8,128)(2,1)S(1)}, bf16[8,48,1536]{2,1,0:T(8,128)(2,1)S(1)}, u32[]{:S(2)}, u32[]{:S(2)}) collective-permute-start(bf16[8,48,1536]{2,1,0:T(8,128)(2,1)S(1)} %add_convert_fusion), channel_id=1, source_target_pairs={{0,2},{1,5},{2,0},{3,7},{4,6},{5,1},{6,4},{7,3},{8,10},{9,13},{10,... | collective-permute-start | bytes 3538952 | tf_op jit(solution)/shard_map/ppermute | solution.py:74
  217.5 14.4 %collective-permute-start.61 = (bf16[1,48,1536]{2,1,0:T(8,128)(2,1)S(1)}, bf16[1,48,1536]{2,1,0:T(8,128)(2,1)S(1)}, u32[]{:S(2)}, u32[]{:S(2)}) collective-permute-start(bf16[1,48,1536]{2,1,0:T(8,128)(2,1)S(1)} %get-tuple-element.169), channel_id=1, source_target_pairs={{0,8},{1,9},{2,10},{3,11},{4,12},{5,13},{6,14},{7,15},{8,16},{9,17... | collective-permute-start | bytes 442376 | tf_op jit(solution)/shard_map/ppermute | solution.py:79
  217.6 14.4 %collective-permute-start.60 = (bf16[1,48,1536]{2,1,0:T(8,128)(2,1)S(1)}, bf16[1,48,1536]{2,1,0:T(8,128)(2,1)S(1)}, u32[]{:S(2)}, u32[]{:S(2)}) collective-permute-start(bf16[1,48,1536]{2,1,0:T(8,128)(2,1)S(1)} %get-tuple-element.200), channel_id=1, source_target_pairs={{0,16},{1,17},{2,18},{3,19},{4,20},{5,21},{6,22},{7,23},{8,24},{9,... | collective-permute-start | bytes 442376 | tf_op jit(solution)/shard_map/ppermute | solution.py:79
  218.7 13.3 %collective-permute-start.59 = (bf16[1,48,1536]{2,1,0:T(8,128)(2,1)S(1)}, bf16[1,48,1536]{2,1,0:T(8,128)(2,1)S(1)}, u32[]{:S(2)}, u32[]{:S(2)}) collective-permute-start(bf16[1,48,1536]{2,1,0:T(8,128)(2,1)S(1)} %get-tuple-element.199), channel_id=1, source_target_pairs={{0,24},{1,25},{2,26},{3,27},{4,28},{5,29},{6,30},{7,31},{8,0},{9,1... | collective-permute-start | bytes 442376 | tf_op jit(solution)/shard_map/ppermute | solution.py:79
  225.8 8.7 %collective-permute-start.44 = (bf16[16,48,1024]{2,1,0:T(8,128)(2,1)}, bf16[16,48,1024]{2,1,0:T(8,128)(2,1)S(1)}, u32[]{:S(2)}, u32[]{:S(2)}) collective-permute-start(bf16[16,48,1024]{2,1,0:T(8,128)(2,1)} %get-tuple-element.178), channel_id=1, source_target_pairs={{0,1},{1,0},{2,3},{3,2},{4,5},{5,4},{6,7},{7,6},{8,9},{9,8},{10,11... | collective-permute-start | bytes 4718600 | tf_op jit(solution)/shard_map/ppermute | solution.py:67
  233.4 11.8 %collective-permute-start.45 = (bf16[4,48,1536]{2,1,0:T(8,128)(2,1)S(1)}, bf16[4,48,1536]{2,1,0:T(8,128)(2,1)S(1)}, u32[]{:S(2)}, u32[]{:S(2)}) collective-permute-start(bf16[4,48,1536]{2,1,0:T(8,128)(2,1)S(1)} %add_convert_fusion.4), channel_id=1, source_target_pairs={{0,4},{1,3},{2,6},{3,1},{4,0},{5,7},{6,2},{7,5},{8,12},{9,11},{10,... | collective-permute-start | bytes 1769480 | tf_op jit(solution)/shard_map/ppermute | solution.py:74
  234.4 17.4 %collective-permute-start.62 = (f32[24,1536]{1,0:T(8,128)S(1)}, f32[24,1536]{1,0:T(8,128)S(1)}, u32[]{:S(2)}, u32[]{:S(2)}) collective-permute-start(f32[24,1536]{1,0:T(8,128)S(1)} %get-tuple-element.230), channel_id=1, source_target_pairs={{0,1},{1,0},{2,3},{3,2},{4,5},{5,4},{6,7},{7,6},{8,9},{9,8},{10,11... | collective-permute-start | bytes 442376 | tf_op jit(solution)/shard_map/ppermute | solution.py:67
  246.7 8.6 %collective-permute-start.65 = (bf16[1,48,1536]{2,1,0:T(8,128)(2,1)S(1)}, bf16[1,48,1536]{2,1,0:T(8,128)(2,1)S(1)}, u32[]{:S(2)}, u32[]{:S(2)}) collective-permute-start(bf16[1,48,1536]{2,1,0:T(8,128)(2,1)S(1)} %get-tuple-element.190), channel_id=1, source_target_pairs={{0,8},{1,9},{2,10},{3,11},{4,12},{5,13},{6,14},{7,15},{8,16},{9,17... | collective-permute-start | bytes 442376 | tf_op jit(solution)/shard_map/ppermute | solution.py:79
  247.3 13.9 %collective-permute-start.64 = (bf16[1,48,1536]{2,1,0:T(8,128)(2,1)S(1)}, bf16[1,48,1536]{2,1,0:T(8,128)(2,1)S(1)}, u32[]{:S(2)}, u32[]{:S(2)}) collective-permute-start(bf16[1,48,1536]{2,1,0:T(8,128)(2,1)S(1)} %get-tuple-element.202), channel_id=1, source_target_pairs={{0,16},{1,17},{2,18},{3,19},{4,20},{5,21},{6,22},{7,23},{8,24},{9,... | collective-permute-start | bytes 442376 | tf_op jit(solution)/shard_map/ppermute | solution.py:79
  248.8 12.4 %collective-permute-start.63 = (bf16[1,48,1536]{2,1,0:T(8,128)(2,1)S(1)}, bf16[1,48,1536]{2,1,0:T(8,128)(2,1)S(1)}, u32[]{:S(2)}, u32[]{:S(2)}) collective-permute-start(bf16[1,48,1536]{2,1,0:T(8,128)(2,1)S(1)} %get-tuple-element.201), channel_id=1, source_target_pairs={{0,24},{1,25},{2,26},{3,27},{4,28},{5,29},{6,30},{7,31},{8,0},{9,1... | collective-permute-start | bytes 442376 | tf_op jit(solution)/shard_map/ppermute | solution.py:79
  251.9 12.1 %collective-permute-start.46 = (bf16[8,48,1024]{2,1,0:T(8,128)(2,1)S(1)}, bf16[8,48,1024]{2,1,0:T(8,128)(2,1)S(1)}, u32[]{:S(2)}, u32[]{:S(2)}) collective-permute-start(bf16[8,48,1024]{2,1,0:T(8,128)(2,1)S(1)} %add_convert_fusion.2), channel_id=1, source_target_pairs={{0,2},{1,5},{2,0},{3,7},{4,6},{5,1},{6,4},{7,3},{8,10},{9,13},{10,... | collective-permute-start | bytes 2359304 | tf_op jit(solution)/shard_map/ppermute | solution.py:74
  252.9 12.1 %collective-permute-start.47 = (bf16[16,48,640]{2,1,0:T(8,128)(2,1)S(1)}, bf16[16,48,640]{2,1,0:T(8,128)(2,1)S(1)}, u32[]{:S(2)}, u32[]{:S(2)}) collective-permute-start(bf16[16,48,640]{2,1,0:T(8,128)(2,1)S(1)} %copy-done.49), channel_id=1, source_target_pairs={{0,1},{1,0},{2,3},{3,2},{4,5},{5,4},{6,7},{7,6},{8,9},{9,8},{10,11... | collective-permute-start | bytes 2949128 | tf_op jit(solution)/shard_map/ppermute | solution.py:67
  262.3 4.0 %collective-permute-start.66 = (f32[24,1536]{1,0:T(8,128)S(1)}, f32[24,1536]{1,0:T(8,128)S(1)}, u32[]{:S(2)}, u32[]{:S(2)}) collective-permute-start(f32[24,1536]{1,0:T(8,128)S(1)} %get-tuple-element.228), channel_id=1, source_target_pairs={{0,1},{1,0},{2,3},{3,2},{4,5},{5,4},{6,7},{7,6},{8,9},{9,8},{10,11... | collective-permute-start | bytes 442376 | tf_op jit(solution)/shard_map/ppermute | solution.py:67
  264.2 11.6 %collective-permute-start.54 = (bf16[4,48,1024]{2,1,0:T(8,128)(2,1)S(1)}, bf16[4,48,1024]{2,1,0:T(8,128)(2,1)S(1)}, u32[]{:S(2)}, u32[]{:S(2)}) collective-permute-start(bf16[4,48,1024]{2,1,0:T(8,128)(2,1)S(1)} %add_convert_fusion.6), channel_id=1, source_target_pairs={{0,4},{1,3},{2,6},{3,1},{4,0},{5,7},{6,2},{7,5},{8,12},{9,11},{10,... | collective-permute-start | bytes 1179656 | tf_op jit(solution)/shard_map/ppermute | solution.py:74
  265.2 15.2 %collective-permute-start.48 = (bf16[8,48,640]{2,1,0:T(8,128)(2,1)S(1)}, bf16[8,48,640]{2,1,0:T(8,128)(2,1)S(1)}, u32[]{:S(2)}, u32[]{:S(2)}) collective-permute-start(bf16[8,48,640]{2,1,0:T(8,128)(2,1)S(1)} %add_convert_fusion.5), channel_id=1, source_target_pairs={{0,2},{1,5},{2,0},{3,7},{4,6},{5,1},{6,4},{7,3},{8,10},{9,13},{10,... | collective-permute-start | bytes 1474568 | tf_op jit(solution)/shard_map/ppermute | solution.py:74
  275.9 6.6 %collective-permute-start.57 = (bf16[1,48,1024]{2,1,0:T(8,128)(2,1)S(1)}, bf16[1,48,1024]{2,1,0:T(8,128)(2,1)S(1)}, u32[]{:S(2)}, u32[]{:S(2)}) collective-permute-start(bf16[1,48,1024]{2,1,0:T(8,128)(2,1)S(1)} %get-tuple-element.198), channel_id=1, source_target_pairs={{0,8},{1,9},{2,10},{3,11},{4,12},{5,13},{6,14},{7,15},{8,16},{9,17... | collective-permute-start | bytes 294920 | tf_op jit(solution)/shard_map/ppermute | solution.py:79
  277.9 7.4 %collective-permute-start.56 = (bf16[1,48,1024]{2,1,0:T(8,128)(2,1)S(1)}, bf16[1,48,1024]{2,1,0:T(8,128)(2,1)S(1)}, u32[]{:S(2)}, u32[]{:S(2)}) collective-permute-start(bf16[1,48,1024]{2,1,0:T(8,128)(2,1)S(1)} %get-tuple-element.197), channel_id=1, source_target_pairs={{0,16},{1,17},{2,18},{3,19},{4,20},{5,21},{6,22},{7,23},{8,24},{9,... | collective-permute-start | bytes 294920 | tf_op jit(solution)/shard_map/ppermute | solution.py:79
  279.6 5.7 %collective-permute-start.55 = (bf16[1,48,1024]{2,1,0:T(8,128)(2,1)S(1)}, bf16[1,48,1024]{2,1,0:T(8,128)(2,1)S(1)}, u32[]{:S(2)}, u32[]{:S(2)}) collective-permute-start(bf16[1,48,1024]{2,1,0:T(8,128)(2,1)S(1)} %get-tuple-element.196), channel_id=1, source_target_pairs={{0,24},{1,25},{2,26},{3,27},{4,28},{5,29},{6,30},{7,31},{8,0},{9,1... | collective-permute-start | bytes 294920 | tf_op jit(solution)/shard_map/ppermute | solution.py:79
  280.4 6.3 %collective-permute-start.49 = (bf16[4,48,640]{2,1,0:T(8,128)(2,1)S(1)}, bf16[4,48,640]{2,1,0:T(8,128)(2,1)S(1)}, u32[]{:S(2)}, u32[]{:S(2)}) collective-permute-start(bf16[4,48,640]{2,1,0:T(8,128)(2,1)S(1)} %add_convert_fusion.7), channel_id=1, source_target_pairs={{0,4},{1,3},{2,6},{3,1},{4,0},{5,7},{6,2},{7,5},{8,12},{9,11},{10,... | collective-permute-start | bytes 737288 | tf_op jit(solution)/shard_map/ppermute | solution.py:74
  285.4 5.9 %collective-permute-start.58 = (f32[24,1024]{1,0:T(8,128)S(1)}, f32[24,1024]{1,0:T(8,128)S(1)}, u32[]{:S(2)}, u32[]{:S(2)}) collective-permute-start(f32[24,1024]{1,0:T(8,128)S(1)} %get-tuple-element.232), channel_id=1, source_target_pairs={{0,1},{1,0},{2,3},{3,2},{4,5},{5,4},{6,7},{7,6},{8,9},{9,8},{10,11... | collective-permute-start | bytes 294920 | tf_op jit(solution)/shard_map/ppermute | solution.py:67
  286.8 6.7 %collective-permute-start.52 = (bf16[1,48,640]{2,1,0:T(8,128)(2,1)S(1)}, bf16[1,48,640]{2,1,0:T(8,128)(2,1)S(1)}, u32[]{:S(2)}, u32[]{:S(2)}) collective-permute-start(bf16[1,48,640]{2,1,0:T(8,128)(2,1)S(1)} %get-tuple-element.223), channel_id=1, source_target_pairs={{0,8},{1,9},{2,10},{3,11},{4,12},{5,13},{6,14},{7,15},{8,16},{9,17... | collective-permute-start | bytes 184328 | tf_op jit(solution)/shard_map/ppermute | solution.py:79
  288.1 7.0 %collective-permute-start.51 = (bf16[1,48,640]{2,1,0:T(8,128)(2,1)S(1)}, bf16[1,48,640]{2,1,0:T(8,128)(2,1)S(1)}, u32[]{:S(2)}, u32[]{:S(2)}) collective-permute-start(bf16[1,48,640]{2,1,0:T(8,128)(2,1)S(1)} %get-tuple-element.224), channel_id=1, source_target_pairs={{0,16},{1,17},{2,18},{3,19},{4,20},{5,21},{6,22},{7,23},{8,24},{9,... | collective-permute-start | bytes 184328 | tf_op jit(solution)/shard_map/ppermute | solution.py:79
  289.3 5.8 %collective-permute-start.50 = (bf16[1,48,640]{2,1,0:T(8,128)(2,1)S(1)}, bf16[1,48,640]{2,1,0:T(8,128)(2,1)S(1)}, u32[]{:S(2)}, u32[]{:S(2)}) collective-permute-start(bf16[1,48,640]{2,1,0:T(8,128)(2,1)S(1)} %get-tuple-element.222), channel_id=1, source_target_pairs={{0,24},{1,25},{2,26},{3,27},{4,28},{5,29},{6,30},{7,31},{8,0},{9,1... | collective-permute-start | bytes 184328 | tf_op jit(solution)/shard_map/ppermute | solution.py:79
  (53 other events, 473.6 us)
